TPU v7x, 256 devices: a whole 4x4x8 slice. The times are simulated.
256 devices in a mesh: depth: 16 (over x, y), row: 2 (over z_hi), col: 8 (over z_lo, core).
Axes of the slice: x: 4, y: 4, z: 8 (z_hi: 2, z_lo: 4; z = z_hi * 4 + z_lo), core: 2. Of those that a mesh axis runs over, the one named last changes fastest.
Arguments:
- inputs: bfloat16 [4608, 4096], P('depth', ('row', 'col')), may hold values from -6 to 6
- gate_weight: bfloat16 [2, 2048, 14336], P('row', 'depth', 'col'), may hold values from -0.09375 to 0.09375
- up_weight: bfloat16 [2, 2048, 14336], P('row', 'depth', 'col'), may hold values from -0.09375 to 0.09375
- cotangent: bfloat16 [4608, 14336], P(('depth', 'row'), 'col'), may hold values from -1.5 to 1.5
Outputs:
- hidden: bfloat16 [4608, 14336], P(('depth', 'row'), 'col')
- input_grad: bfloat16 [4608, 4096], P('depth', ('row', 'col'))
- gate_grad: bfloat16 [2, 2048, 14336], P('row', 'depth', 'col')
- up_grad: bfloat16 [2, 2048, 14336], P('row', 'depth', 'col')
All inputs are finite; a program needn't handle non-finite values.
Results may differ from a plain program's by a relative error of at most 0.024.
Values may be sent and summed in bfloat16 or wider, within the bound.
A program may use at most 128 MiB of HBM per device.

v0:
```python
import jax
import jax.numpy as jnp
from jax import lax
from jax.sharding import PartitionSpec as P


def delta_terms(gate_sum, up_sum, upstream_bf):
    sig = jax.nn.sigmoid(gate_sum)
    act = gate_sum * sig
    upstream = upstream_bf.astype(jnp.float32)
    up_delta = (upstream * act).astype(jnp.bfloat16)
    gate_delta = (upstream * up_sum * sig * (1.0 + gate_sum * (1.0 - sig))).astype(jnp.bfloat16)
    return (act, gate_delta, up_delta)


def local(inputs, gate_weight, up_weight, cotangent):
    panel = lax.all_gather(inputs, "col", axis=1, tiled=True)
    gate_stack, up_stack = (
        lax.all_gather(gate_weight, "depth", axis=1, tiled=True),
        lax.all_gather(up_weight, "depth", axis=1, tiled=True),
    )
    gate_panel = gate_stack[0]
    up_panel = up_stack[0]
    gate_part = jnp.dot(panel, gate_panel, preferred_element_type=jnp.float32)
    up_part = jnp.dot(panel, up_panel, preferred_element_type=jnp.float32)
    gate_sum, up_sum = (
        lax.psum_scatter(
            gate_part.astype(jnp.bfloat16), "row", scatter_dimension=0, tiled=True
        ).astype(jnp.float32),
        lax.psum_scatter(
            up_part.astype(jnp.bfloat16), "row", scatter_dimension=0, tiled=True
        ).astype(jnp.float32),
    )
    act, gate_share, up_share = delta_terms(gate_sum, up_sum, cotangent)
    hidden = (act * up_sum).astype(jnp.bfloat16)
    gate_delta, up_delta = (
        lax.all_gather(gate_share, "row", axis=0, tiled=True),
        lax.all_gather(up_share, "row", axis=0, tiled=True),
    )
    dims = (((1,), (1,)), ((), ()))
    input_part = lax.dot_general(gate_delta, gate_panel, dims, preferred_element_type=jnp.float32)
    input_part = input_part + lax.dot_general(
        up_delta, up_panel, dims, preferred_element_type=jnp.float32
    )
    input_grad = lax.psum_scatter(
        input_part.astype(jnp.bfloat16), "col", scatter_dimension=1, tiled=True
    )
    deltas = jnp.concatenate((gate_delta, up_delta), axis=1)
    summed = lax.psum_scatter(
        lax.dot_general(
            panel, deltas, (((0,), (0,)), ((), ())), preferred_element_type=jnp.float32
        ).astype(jnp.bfloat16),
        "depth",
        scatter_dimension=0,
        tiled=True,
    ).astype(jnp.float32)
    width = gate_panel.shape[1]
    gate_grad = summed[:, :width].astype(jnp.bfloat16)[None]
    up_grad = summed[:, width:].astype(jnp.bfloat16)[None]
    return (hidden, input_grad, gate_grad, up_grad)


def solution(mesh):
    return jax.shard_map(
        local,
        mesh=mesh,
        in_specs=(
            P("depth", ("row", "col")),
            P("row", "depth", "col"),
            P("row", "depth", "col"),
            P(("depth", "row"), "col"),
        ),
        out_specs=(
            P(("depth", "row"), "col"),
            P("depth", ("row", "col")),
            P("row", "depth", "col"),
            P("row", "depth", "col"),
        ),
        check_vma=False,
    )
```

profile of v0, /device:TPU:32, one launch (start us, length us, event | category | flops | bytes accessed | tf_op | source)
XLA Modules:
  0.0 507.1 jit_solution(6634828496853838766)
XLA Ops:
  7.2 0.0 all-gather.4.cloned.1.call-start
  7.2 0.7 all-gather.4.cloned.1.call-update
  7.9 0.0 all-gather.8.cloned.1.call-start
  7.9 0.7 all-gather.8.cloned.1.call-update
  8.6 0.0 all-gather.6.cloned.1.call-start
  8.7 0.7 all-gather.6.cloned.1.call-update
  9.4 0.0 reduce-scatter.9.cloned.1.call-start
  9.4 34.8 %all-gather.4.cloned.1.call-done = bf16[288,2048]{1,0:T(8,128)(2,1)} async-done(((bf16[288,256]{1,0:T(8,128)(2,1)}), bf16[288,2048]{1,0:T(8,128)(2,1)}) %all-gather.4.cloned.1.call-update) | async-done | bytes 1179664 | tf_op jit(solution)/shard_map/all_gather | solution.py:17
  44.3 0.0 copy-start.1
  44.3 74.1 %all-gather.8.cloned.1.call-done = bf16[1,2048,1792]{2,1,0:T(8,128)(2,1)} async-done(((bf16[1,128,1792]{2,1,0:T(8,128)(2,1)}), bf16[1,2048,1792]{2,1,0:T(8,128)(2,1)}) %all-gather.8.cloned.1.call-update) | async-done | bytes 7340048 | tf_op jit(solution)/shard_map/all_gather | solution.py:20
  118.4 6.7 %fusion.18 = bf16[288,1792]{1,0:T(8,128)(2,1)} fusion(bf16[288,2048]{1,0:T(8,128)(2,1)} %all-gather.4.cloned.1.call-done, bf16[1,2048,1792]{2,1,0:T(8,128)(2,1)} %all-gather.8.cloned.1.call-done), kind=kOutput, calls=%fused_computation.13 | convolution fusion | flops 2114445312 | bytes 9551872 | tf_op jit(solution)/shard_map/dot_general | solution.py:25
  125.1 0.0 reduce-scatter.9.cloned.1.call-update
  125.1 0.0 copy-start
  125.1 0.0 reduce-scatter.7.cloned.1.call-start
  125.2 66.6 %all-gather.6.cloned.1.call-done = bf16[1,2048,1792]{2,1,0:T(8,128)(2,1)} async-done(((bf16[1,128,1792]{2,1,0:T(8,128)(2,1)}), bf16[1,2048,1792]{2,1,0:T(8,128)(2,1)}) %all-gather.6.cloned.1.call-update) | async-done | bytes 7340048 | tf_op jit(solution)/shard_map/all_gather | solution.py:19
  191.8 0.0 copy-done.1
  191.8 6.3 %fusion.15 = bf16[288,1792]{1,0:T(8,128)(2,1)} fusion(bf16[288,2048]{1,0:T(8,128)(2,1)S(1)} %copy-done.1, bf16[1,2048,1792]{2,1,0:T(8,128)(2,1)} %all-gather.6.cloned.1.call-done), kind=kOutput, calls=%fused_computation.12 | convolution fusion | flops 2114445312 | bytes 9551872 | tf_op jit(solution)/shard_map/dot_general | solution.py:24
  198.1 0.0 reduce-scatter.7.cloned.1.call-update
  198.2 0.0 reduce-scatter.13.cloned.1.call-start
  198.2 35.3 %reduce-scatter.9.cloned.1.call-done = bf16[144,1792]{1,0:T(8,128)(2,1)} async-done(((bf16[288,1792]{1,0:T(8,128)(2,1)}), bf16[144,1792]{1,0:T(8,128)(2,1)}) %reduce-scatter.9.cloned.1.call-update) | async-done | bytes 516112 | tf_op jit(solution)/shard_map/reduce_scatter | solution.py:30
  233.5 39.4 %reduce-scatter.7.cloned.1.call-done = bf16[144,1792]{1,0:T(8,128)(2,1)} async-done(((bf16[288,1792]{1,0:T(8,128)(2,1)}), bf16[144,1792]{1,0:T(8,128)(2,1)}) %reduce-scatter.7.cloned.1.call-update) | async-done | bytes 516112 | tf_op jit(solution)/shard_map/reduce_scatter | solution.py:27
  272.9 0.0 copy-done
  272.9 2.6 fusion.27
  275.5 27.4 %all_gather.18 = bf16[288,1792]{1,0:T(8,128)(2,1)S(1)} all-gather(bf16[144,1792]{1,0:T(8,128)(2,1)S(1)} %get-tuple-element.12), channel_id=1, replica_groups=mesh['depth'=16,'row'=2,'col'=8] {'row'}, dimensions={0}, use_global_device_ids=true | all-gather | bytes 1548288 | tf_op jit(solution)/shard_map/all_gather | solution.py:37
  302.9 24.1 %all_gather.19 = bf16[288,1792]{1,0:T(8,128)(2,1)S(1)} all-gather(bf16[144,1792]{1,0:T(8,128)(2,1)S(1)} %get-tuple-element.13), channel_id=1, replica_groups=mesh['depth'=16,'row'=2,'col'=8] {'row'}, dimensions={0}, use_global_device_ids=true | all-gather | bytes 1548288 | tf_op jit(solution)/shard_map/all_gather | solution.py:38
  327.0 11.1 %fusion = bf16[2048,3584]{0,1:T(8,128)(2,1)} fusion(bf16[288,2048]{1,0:T(8,128)(2,1)S(1)} %copy-done.1, bf16[288,1792]{1,0:T(8,128)(2,1)S(1)} %all_gather.19, bf16[288,1792]{1,0:T(8,128)(2,1)S(1)} %all_gather.18), kind=kOutput, calls=%fused_computation.1 | convolution fusion | flops 4239327232 | bytes 17924096 | tf_op jit(solution)/shard_map/dot_general | solution.py:50
  338.0 18.8 %copy.12 = bf16[2048,3584]{1,0:T(8,128)(2,1)} copy(bf16[2048,3584]{0,1:T(8,128)(2,1)} %fusion) | data formatting | bytes 29360128
  356.8 0.0 reduce-scatter.13.cloned.1.call-update
  356.8 0.2 reduce-scatter.11.cloned.1.call-start
  357.1 5.4 %fusion.1 = f32[288,2048]{1,0:T(8,128)S(1)} fusion(bf16[288,1792]{1,0:T(8,128)(2,1)S(1)} %all_gather.19, bf16[1,2048,1792]{2,1,0:T(8,128)(2,1)} %all-gather.8.cloned.1.call-done), kind=kOutput, calls=%fused_computation.2 | convolution fusion | flops 2113929216 | bytes 10731520 | tf_op jit(solution)/shard_map/dot_general | solution.py:42
  362.5 6.4 %fusion.12 = bf16[288,2048]{1,0:T(8,128)(2,1)} fusion(f32[288,2048]{1,0:T(8,128)S(1)} %fusion.1, bf16[288,1792]{1,0:T(8,128)(2,1)S(1)} %all_gather.18, bf16[1,2048,1792]{2,1,0:T(8,128)(2,1)} %all-gather.6.cloned.1.call-done), kind=kOutput, calls=%fused_computation.11 | convolution fusion | flops 2115108864 | bytes 11911168 | tf_op jit(solution)/shard_map/dot_general | solution.py:41
  368.9 0.0 reduce-scatter.11.cloned.1.call-update
  369.0 95.1 %reduce-scatter.13.cloned.1.call-done = bf16[128,3584]{1,0:T(8,128)(2,1)} async-done(((bf16[2048,3584]{1,0:T(8,128)(2,1)}), bf16[128,3584]{1,0:T(8,128)(2,1)}) %reduce-scatter.13.cloned.1.call-update) | async-done | bytes 917520
  464.1 1.2 fusion.34
  465.3 0.3 copy.15
  465.6 1.0 copy.11
  466.5 0.3 copy.14
  466.8 1.0 copy.10
  467.8 32.5 %reduce-scatter.11.cloned.1.call-done = bf16[288,256]{1,0:T(8,128)(2,1)} async-done(((bf16[288,2048]{1,0:T(8,128)(2,1)}), bf16[288,256]{1,0:T(8,128)(2,1)}) %reduce-scatter.11.cloned.1.call-update) | async-done | bytes 147472 | tf_op jit(solution)/shard_map/reduce_scatter | solution.py:45
Async XLA Ops:
  7.2 37.1 %all-gather.4.cloned.1.call-start = ((), (), s32[]{:S(2)}) async-start(), calls=%async_computation.4 | async-start | bytes 1327104 | tf_op jit(solution)/shard_map/all_gather | solution.py:17
  7.9 110.5 %all-gather.8.cloned.1.call-start = ((), (), s32[]{:S(2)}) async-start(), calls=%async_computation.7 | async-start | bytes 7798784 | tf_op jit(solution)/shard_map/all_gather | solution.py:20
  8.6 183.1 %all-gather.6.cloned.1.call-start = ((), (), s32[]{:S(2)}) async-start(), calls=%async_computation.5 | async-start | bytes 7798784 | tf_op jit(solution)/shard_map/all_gather | solution.py:19
  9.4 224.2 %reduce-scatter.9.cloned.1.call-start = ((), (), s32[]{:S(2)}) async-start(), calls=%async_computation.8 | async-start | bytes 1548288 | tf_op jit(solution)/shard_map/reduce_scatter | solution.py:30
  44.3 147.5 %copy-start.1 = (bf16[288,2048]{1,0:T(8,128)(2,1)S(1)}, bf16[288,2048]{1,0:T(8,128)(2,1)}, u32[]{:S(2)}) copy-start(bf16[288,2048]{1,0:T(8,128)(2,1)} %all-gather.4.cloned.1.call-done) | copy-start | bytes 3538948
  125.1 147.8 %copy-start = (bf16[144,1792]{1,0:T(8,128)(2,1)S(1)}, bf16[144,1792]{1,0:T(8,128)(2,1)}, u32[]{:S(2)}) copy-start(bf16[144,1792]{1,0:T(8,128)(2,1)} %param.7) | copy-start | bytes 1548292
  125.1 147.8 %reduce-scatter.7.cloned.1.call-start = ((), (), s32[]{:S(2)}) async-start(), calls=%async_computation.6 | async-start | bytes 1548288 | tf_op jit(solution)/shard_map/reduce_scatter | solution.py:27
  198.2 265.9 %reduce-scatter.13.cloned.1.call-start = ((), (), s32[]{:S(2)}) async-start(), calls=%async_computation.10 | async-start | bytes 15597568
  356.8 143.4 %reduce-scatter.11.cloned.1.call-start = ((), (), s32[]{:S(2)}) async-start(), calls=%async_computation.9 | async-start | bytes 1327104 | tf_op jit(solution)/shard_map/reduce_scatter | solution.py:45
Sparse Core Ops, SparseCore 0:
  9.7 34.5 all-gather.3
  46.7 71.5 all-gather.7
  120.8 70.8 all-gather.5
  194.2 39.3 reduce-scatter.8
  235.9 36.9 reduce-scatter.6
  357.0 107.0 reduce-scatter.12
  467.2 33.0 reduce-scatter.10
where the time goes:
time: 512 us; the launch traced here: 507 us
  waiting for transfers between devices  380 us (74%)
  blocking collectives  51.4 us (10%)
  matrix products  36 us (7%)
  local copies, waits for them, and re-layouts  22.5 us (4%)
  between operations  14.2 us (3%)
    unnamed x8, waiting for transfers between devices  97.2 us
    all_gather x1, waiting for transfers between devices, local(): lax.all_gather(up_weight, 'depth', axis=1, tiled=True)  74.1 us
    all_gather x1, waiting for transfers between devices, local(): lax.all_gather(gate_weight, 'depth', axis=1, tiled=True)  66.6 us
    reduce_scatter x1, waiting for transfers between devices, local(): lax.psum_scatter(gate_part.astype(jnp.bfloat16), 'row', scatter_dimension...  39.4 us
    reduce_scatter x1, waiting for transfers between devices, local(): lax.psum_scatter(up_part.astype(jnp.bfloat16), 'row', scatter_dimension=0...  35.3 us
    all_gather x1, waiting for transfers between devices, local(): panel = lax.all_gather(inputs, 'col', axis=1, tiled=True)  34.8 us
    reduce_scatter x1, waiting for transfers between devices, local(): lax.psum_scatter(input_part.astype(jnp.bfloat16), 'col', scatter_dimensio...  32.5 us
    all_gather x1, blocking collectives, local(): lax.all_gather(gate_share, 'row', axis=0, tiled=True)  27.4 us
  transfers between devices with their start and end apart: 7, of which 7 were waited for; matrix products, arithmetic and copies ran while one was open for 6% of the time, Pallas kernels for 0%

commit v1 on v0

v1 whole, which is shorter than its diff:
```python
import functools

import jax
import jax.numpy as jnp
from jax import lax
from jax.experimental import pallas as pl
from jax.experimental.pallas import tpu as pltpu
from jax.sharding import PartitionSpec as P

MESH = pl.DeviceIdType.MESH
BF = jnp.bfloat16
F32 = jnp.float32
NX = 4
ROWS = 128
CW = 128
TICKS_TO_FORWARD = 4


def kernel(
    nch, x_hbm, gw_hbm, uw_hbm, cot_hbm, hid_ref, dx_ref, gg_ref, ug_ref,
    panel, gpart, rb0, rb1, rb2, rb3, xp, xt, acc, part, zin, dl, cot, dxs, dxr, dxz, dxq,
    loc_sem, in_sem, ag_send, ag_recv, rs_send, rs_recv, z_send, z_recv, x_send, x_recv, d_send, d_recv,
):
    d, r, c = lax.axis_index("depth"), lax.axis_index("row"), lax.axis_index("col")
    x, y = lax.div(d, NX), lax.rem(d, NX)
    zl, k = lax.div(c, 2), lax.rem(c, 2)
    tok = dx_ref.shape[0]
    half = tok // 2
    fb = dx_ref.shape[1]

    def ring(p, s):
        return lax.rem(p + s + NX, NX)

    def x_dev(s):
        return {"depth": ring(x, s) * NX + y}

    def y_dev(s):
        return {"depth": x * NX + ring(y, s)}

    row_dev = {"row": 1 - r}
    sib_dev = {"col": c + 1 - 2 * k}

    def z_dev(s):
        return {"col": ring(zl, s) * 2 + k}

    def remote(src, dst, ssem, rsem, dev):
        return pltpu.make_async_remote_copy(
            src_ref=src, dst_ref=dst, send_sem=ssem, recv_sem=rsem, device_id=dev, device_id_type=MESH
        )

    def cols(j):
        return pl.ds(pl.multiple_of(j * CW, CW), CW)

    def feat(b):
        return pl.ds(pl.multiple_of(b * fb, fb), fb)

    w_hbm = (gw_hbm, uw_hbm)

    def own(j, s):
        return pltpu.make_async_copy(w_hbm[s].at[0, :, cols(j)], panel.at[j, s, x, y], loc_sem.at[s, j])

    own_x = pltpu.make_async_copy(x_hbm, xp.at[:, feat(c)], in_sem.at[0])
    own_cot = pltpu.make_async_copy(cot_hbm, cot, in_sem.at[1])

    def start_own(j, carry):
        for s in range(2):
            own(j, s).start()
        return carry

    own_x.start()
    lax.fori_loop(0, nch, start_own, 0)
    own_cot.start()

    partners = [x_dev(1), x_dev(-1), y_dev(1), y_dev(-1), row_dev, sib_dev, z_dev(1), z_dev(2), z_dev(3)]
    barrier = pltpu.get_barrier_semaphore()
    for dev in partners:
        pl.semaphore_signal(barrier, inc=1, device_id=dev, device_id_type=MESH)
    pl.semaphore_wait(barrier, len(partners))

    def x_line(s, b):
        blk = xp.at[:, feat(b)]
        return remote(blk, blk, x_send.at[s - 1], x_recv.at[s - 1], z_dev(s))

    def x_sib(s, b):
        blk = xp.at[:, feat(b)]
        return remote(blk, blk, x_send.at[3 + s], x_recv.at[3 + s], sib_dev)

    def x_start():
        own_x.wait()
        for s in (1, 2, 3):
            x_line(s, c).start()
        x_sib(0, c).start()

    def x_forward():
        for s in (1, 3, 2):
            b = ring(zl, -s) * 2 + k
            x_line(s, b).wait_recv()
            x_sib(s, b).start()

    def x_finish():
        for s in (1, 2, 3):
            x_line(s, c).wait_send()
        for s in range(4):
            b = ring(zl, -s) * 2 + 1 - k
            x_sib(s, b).wait_recv()
            x_sib(s, c).wait_send()
        for i in range(NX):
            w = 4 * ROWS
            xt[i] = jnp.transpose(xp[:, i * w : (i + 1) * w])

    def ring_dev(axis, s):
        return x_dev(s) if axis == 0 else y_dev(s)

    def me(axis):
        return x if axis == 0 else y

    def block(buf, j, s, p):
        return buf.at[j, 0, p, y] if s == 0 else buf.at[j, 1, x, p]

    def block_half(buf, j, s, p, h):
        rows = pl.ds(h * (ROWS // 2), ROWS // 2)
        return buf.at[j, 0, p, y, rows] if s == 0 else buf.at[j, 1, x, p, rows]

    def group(buf, j, s, q):
        return buf.at[j, 0, :, q] if s == 0 else buf.at[j, 1, q]

    def group_half(buf, j, s, q, h):
        return buf.at[j, 0, pl.ds(2 * h, 2), q] if s == 0 else buf.at[j, 1, q, pl.ds(2 * h, 2)]

    def ag(stage, j, s, i, src):
        axis = s if stage < 2 else 1 - s
        return remote(
            src, src, ag_send.at[stage, s, i, j], ag_recv.at[stage, s, i, j], ring_dev(axis, 1 - 2 * i)
        )

    def ag0(j):
        for s in range(2):
            own(j, s).wait()
        for s in range(2):
            for i in range(2):
                ag(0, j, s, i, block(panel, j, s, me(s))).start()

    def ag1(j):
        for s in range(2):
            m = me(s)
            for i in range(2):
                src = ring(m, -1 + 2 * i)
                ag(0, j, s, i, block(panel, j, s, src)).wait_recv()
                ag(1, j, s, i, block_half(panel, j, s, src, i)).start()
        for s in range(2):
            for i in range(2):
                ag(0, j, s, i, block(panel, j, s, me(s))).wait_send()

    def ag2(j):
        for s in range(2):
            m = me(s)
            for i in range(2):
                ag(1, j, s, i, block_half(panel, j, s, ring(m, 2), i)).wait_recv()
            for i in range(2):
                ag(2, j, s, i, group(panel, j, s, me(1 - s))).start()
        for s in range(2):
            for i in range(2):
                ag(1, j, s, i, block_half(panel, j, s, me(s), i)).wait_send()

    def ag3(j):
        for s in range(2):
            m = me(1 - s)
            for i in range(2):
                src = ring(m, -1 + 2 * i)
                ag(2, j, s, i, group(panel, j, s, src)).wait_recv()
                ag(3, j, s, i, group_half(panel, j, s, src, i)).start()
        for s in range(2):
            for i in range(2):
                ag(2, j, s, i, group(panel, j, s, me(1 - s))).wait_send()

    def ag4(j):
        for s in range(2):
            m = me(1 - s)
            for i in range(2):
                ag(3, j, s, i, group_half(panel, j, s, ring(m, 2), i)).wait_recv()
        for s in range(2):
            for i in range(2):
                ag(3, j, s, i, group_half(panel, j, s, me(1 - s), i)).wait_send()

    def z1(j, src):
        return remote(src, zin.at[j], z_send.at[0, j], z_recv.at[0, j], row_dev)

    def z2(j, h):
        return remote(dl.at[j, h], dl.at[j, h], z_send.at[1, j], z_recv.at[1, j], row_dev)

    def weights(j, i):
        n = 4 * ROWS
        return jnp.concatenate([panel[j, 0, i].reshape(n, CW), panel[j, 1, i].reshape(n, CW)], axis=1)

    def forward(j):
        ag4(j)
        w = jnp.concatenate([weights(j, i) for i in range(NX)], axis=0)
        out = jnp.dot(xp[...], w, preferred_element_type=F32)
        part[j] = out.reshape(2, half, 2 * CW).astype(BF)
        z1(j, part.at[j, 1 - r]).start()

    def deltas(j):
        z1(j, part.at[j, 1 - r]).wait()
        total = part[j, r].astype(F32) + zin[j].astype(F32)
        gate, up = total[:, :CW], total[:, CW:]
        sig = jax.nn.sigmoid(gate)
        act = gate * sig
        hid_ref[:, cols(j)] = (act * up).astype(BF)
        upstream = cot[:, cols(j)].astype(F32)
        gd = (upstream * up * sig * (1.0 + gate * (1.0 - sig))).astype(BF)
        ud = (upstream * act).astype(BF)
        dl[j, r] = jnp.concatenate([gd, ud], axis=1)
        z2(j, r).start()

    def grads(j):
        z2(j, 1 - r).wait_recv()
        z2(j, r).wait_send()

        def wgrad(i, carry):
            g = jnp.dot(xt[i], dl[j].reshape(tok, 2 * CW), preferred_element_type=F32).astype(BF)
            gpart[j, 0, i] = g[:, :CW].reshape(NX, ROWS, CW)
            gpart[j, 1, i] = g[:, CW:].reshape(NX, ROWS, CW)
            return carry

        lax.fori_loop(0, NX, wgrad, 0)
        rs0(j)

        def dgrad(i, carry):
            w = weights(j, i)
            p = lax.dot_general(
                dl[j].reshape(tok, 2 * CW), w, (((1,), (1,)), ((), ())), preferred_element_type=F32
            )
            sl = pl.ds(pl.multiple_of(i * 4 * ROWS, 4 * ROWS), 4 * ROWS)

            @pl.when(j == 0)
            def _():
                acc[:, sl] = p

            @pl.when(j > 0)
            def _():
                acc[:, sl] += p

            return carry

        lax.fori_loop(0, NX, dgrad, 0)

    def rs(stage, j, s, i, src):
        axis = 1 - s if stage < 2 else s
        dst = (rb0, rb1, rb2, rb3)[stage].at[j, s, i]
        return remote(src, dst, rs_send.at[stage, s, i, j], rs_recv.at[stage, s, i, j], ring_dev(axis, 1 - 2 * i))

    def add(ref, *others):
        v = ref[...].astype(F32)
        for o in others:
            v = v + o[...].astype(F32)
        ref[...] = v.astype(BF)

    def rs0(j):
        for s in range(2):
            far = ring(me(1 - s), 2)
            for i in range(2):
                rs(0, j, s, i, group_half(gpart, j, s, far, i)).start()

    def rs1(j):
        for s in range(2):
            m = me(1 - s)
            for i in range(2):
                rs(0, j, s, i, group_half(gpart, j, s, ring(m, 2), i)).wait_recv()
                near = ring(m, 1 - 2 * i)
                add(group_half(gpart, j, s, near, i), rb0.at[j, s, i])
                rs(1, j, s, i, group(gpart, j, s, near)).start()
        for s in range(2):
            for i in range(2):
                rs(0, j, s, i, group_half(gpart, j, s, ring(me(1 - s), 2), i)).wait_send()

    def rs2(j):
        for s in range(2):
            m = me(1 - s)
            mine = group(gpart, j, s, m)
            for i in range(2):
                rs(1, j, s, i, mine).wait_recv()
            add(mine, rb1.at[j, s, 0], rb1.at[j, s, 1])
            far = ring(me(s), 2)
            for i in range(2):
                rs(2, j, s, i, block_half(gpart, j, s, far, i)).start()
        for s in range(2):
            for i in range(2):
                rs(1, j, s, i, group(gpart, j, s, ring(me(1 - s), 1 - 2 * i))).wait_send()

    def rs3(j):
        for s in range(2):
            m = me(s)
            for i in range(2):
                rs(2, j, s, i, block_half(gpart, j, s, ring(m, 2), i)).wait_recv()
                near = ring(m, 1 - 2 * i)
                add(block_half(gpart, j, s, near, i), rb2.at[j, s, i])
                rs(3, j, s, i, block(gpart, j, s, near)).start()
        for s in range(2):
            for i in range(2):
                rs(2, j, s, i, block_half(gpart, j, s, ring(me(s), 2), i)).wait_send()

    def rs4(j):
        for s, out in enumerate((gg_ref, ug_ref)):
            mine = block(gpart, j, s, me(s))
            for i in range(2):
                rs(3, j, s, i, mine).wait_recv()
            v = mine[...].astype(F32) + rb3[j, s, 0].astype(F32) + rb3[j, s, 1].astype(F32)
            out[0, :, cols(j)] = v.astype(BF)
        for s in range(2):
            for i in range(2):
                rs(3, j, s, i, block(gpart, j, s, ring(me(s), 1 - 2 * i))).wait_send()

    d_sib = remote(dxs, dxr, d_send.at[0], d_recv.at[0], sib_dev)

    def d_line(s):
        return remote(dxz.at[s - 1], dxq.at[s - 1], d_send.at[s], d_recv.at[s], z_dev(s))

    def dx0():
        for i in range(4):
            dxs[i] = acc[:, feat(2 * i + 1 - k)].astype(BF)
        d_sib.start()

    def dx1():
        d_sib.wait()
        for s in (2, 1, 3):
            zt = ring(zl, s)
            dxz[s - 1] = (acc[:, feat(2 * zt + k)] + dxr[zt].astype(F32)).astype(BF)
            d_line(s).start()

    def dx2():
        v = acc[:, feat(2 * zl + k)] + dxr[zl].astype(F32)
        for s in (1, 2, 3):
            d_line(s).wait()
            v = v + dxq[s - 1].astype(F32)
        dx_ref[...] = v.astype(BF)

    x_start()
    fo = TICKS_TO_FORWARD

    def tick(t, carry):
        def at(off, fn):
            j = t - off

            @pl.when((j >= 0) & (j < nch))
            def _():
                fn(j)

        at(3, ag3)
        at(2, ag2)
        at(1, ag1)
        at(0, ag0)
        pl.when(t == 1)(x_forward)

        @pl.when(t == 3)
        def _():
            x_finish()
            own_cot.wait()

        at(fo + 6, rs4)
        at(fo + 5, rs3)
        at(fo + 4, rs2)
        at(fo + 3, rs1)
        at(fo + 1, deltas)
        at(fo, forward)
        at(fo + 2, grads)
        pl.when(t == nch + fo + 1)(dx0)
        pl.when(t == nch + fo + 2)(dx1)
        pl.when(t == nch + fo + 4)(dx2)
        return carry

    lax.fori_loop(0, nch + fo + 6, tick, 0)


def local(inputs, gate_weight, up_weight, cotangent):
    tok, fb = inputs.shape
    _, rows, width = gate_weight.shape
    half = cotangent.shape[0]
    nch = width // CW
    feats = rows * NX * NX
    vm, dma = pltpu.VMEM, pltpu.SemaphoreType.DMA
    any_spec = pl.BlockSpec(memory_space=pl.ANY)
    vmem_spec = pl.BlockSpec(memory_space=pltpu.VMEM)
    return pl.pallas_call(
        functools.partial(kernel, nch),
        out_shape=(
            jax.ShapeDtypeStruct((half, width), BF),
            jax.ShapeDtypeStruct((tok, fb), BF),
            jax.ShapeDtypeStruct((1, rows, width), BF),
            jax.ShapeDtypeStruct((1, rows, width), BF),
        ),
        in_specs=[any_spec] * 4,
        out_specs=[vmem_spec] * 4,
        scratch_shapes=[
            vm((nch, 2, NX, NX, rows, CW), BF),
            vm((nch, 2, NX, NX, rows, CW), BF),
            vm((nch, 2, 2, 2, rows, CW), BF),
            vm((nch, 2, 2, NX, rows, CW), BF),
            vm((nch, 2, 2, rows // 2, CW), BF),
            vm((nch, 2, 2, rows, CW), BF),
            vm((tok, feats), BF),
            vm((NX, 4 * rows, tok), BF),
            vm((tok, feats), F32),
            vm((nch, 2, half, 2 * CW), BF),
            vm((nch, half, 2 * CW), BF),
            vm((nch, 2, half, 2 * CW), BF),
            vm((half, width), BF),
            vm((4, tok, fb), BF),
            vm((4, tok, fb), BF),
            vm((3, tok, fb), BF),
            vm((3, tok, fb), BF),
            dma((2, nch)),
            dma((2,)),
            dma((4, 2, 2, nch)),
            dma((4, 2, 2, nch)),
            dma((4, 2, 2, nch)),
            dma((4, 2, 2, nch)),
            dma((2, nch)),
            dma((2, nch)),
            dma((7,)),
            dma((7,)),
            dma((4,)),
            dma((4,)),
        ],
        compiler_params=pltpu.CompilerParams(
            collective_id=0, has_side_effects=True, vmem_limit_bytes=62 * 2**20
        ),
    )(inputs, gate_weight, up_weight, cotangent)


def solution(mesh):
    return jax.shard_map(
        local,
        mesh=mesh,
        in_specs=(
            P("depth", ("row", "col")),
            P("row", "depth", "col"),
            P("row", "depth", "col"),
            P(("depth", "row"), "col"),
        ),
        out_specs=(
            P(("depth", "row"), "col"),
            P("depth", ("row", "col")),
            P("row", "depth", "col"),
            P("row", "depth", "col"),
        ),
        check_vma=False,
    )
```

time: 512 us -> 206 us (0.40)
  waiting for transfers between devices: 380 us -> 0 us
  Pallas kernels: 0 us -> 201 us
  blocking collectives: 51.4 us -> 0 us
  matrix products: 36 us -> 0 us
  local copies, waits for them, and re-layouts: 22.5 us -> 4.54 us
  between operations: 14.2 us -> 0.66 us
    pallas_call x0 -> x1, Pallas kernels: none -> 201 us  [local(): pl.pallas_call(functools.partial(kernel, nch), out_shape=(jax.ShapeDtypeS...]
    all_gather x3 -> x0, waiting for transfers between devices: 176 us -> none  [the longest x1 74.1 us: local(): lax.all_gather(up_weight, 'depth', axis=1, tiled=True)]
    reduce_scatter x3 -> x0, waiting for transfers between devices: 107 us -> none  [the longest x1 39.4 us: local(): lax.psum_scatter(gate_part.astype(jnp.bfloat16), 'row', scatter_dimension...]
    unnamed x8 -> x0, waiting for transfers between devices: 97.2 us -> none
    all_gather x2 -> x0, blocking collectives: 51.4 us -> none  [the longest x1 27.4 us: local(): lax.all_gather(gate_share, 'row', axis=0, tiled=True)]
    dot_general x5 -> x0, matrix products: 36 us -> none  [the longest x1 11.1 us: local(): lax.dot_general(panel, deltas, (((0,), (0,)), ((), ())), preferred_elemen...]
    unnamed x9 -> x10, local copies, waits for them, and re-layouts: 21.3 us -> 4.54 us
  transfers between devices with their start and end apart: 7 -> 0, of which waited for: 7 -> 0; matrix products, arithmetic and copies ran while one was open for 6% -> 0% of each run, Pallas kernels for 0% -> 0%
where the time goes in v1:
time: 206 us
  Pallas kernels  201 us (98%)
  local copies, waits for them, and re-layouts  4.54 us (2%)
    pallas_call x1, Pallas kernels, local(): pl.pallas_call(functools.partial(kernel, nch), out_shape=(jax.ShapeDtypeS...  201 us
    unnamed x10, local copies, waits for them, and re-layouts  4.54 us

profile of v1, /device:TPU:32, one launch (start us, length us, event | category | flops | bytes accessed | tf_op | source)
XLA Modules:
  0.0 206.2 jit_solution(5027397556442400432)
XLA Ops:
  0.6 201.0 %shard_map.75 = (bf16[144,1792]{1,0:T(8,128)(2,1)}, bf16[288,256]{1,0:T(8,128)(2,1)}, bf16[1,128,1792]{2,1,0:T(8,128)(2,1)}, bf16[1,128,1792]{2,1,0:T(8,128)(2,1)}) custom-call(bf16[288,256]{1,0:T(8,128)(2,1)} %x_hbm.1, bf16[1,128,1792]{2,1,0:T(8,128)(2,1)} %gw_hbm.1, bf16[1,128,1792]{2,1,0:T(8,128)(2,1)} %uw_hbm.1, bf16[144,1792]{1,0:T(8,128)(2,1)} %cot_hbm.1), custom_call_target="tpu_custom_call" | custom-call | tf_op jit(solution)/shard_map/pallas_call | solution.py:383
  201.7 0.0 copy-start.2
  201.7 0.0 copy-start.1
  201.7 1.9 copy.12
  203.6 0.0 copy-done.2
  203.6 0.7 copy.13
  204.3 0.0 copy-done.1
  204.3 0.0 copy-start
  204.3 0.8 copy.14
  205.0 0.4 copy-done
  205.5 0.8 copy.15
Async XLA Ops:
  201.7 1.9 copy-start.2
  201.7 2.6 %copy-start.1 = (bf16[1,128,1792]{2,1,0:T(8,128)(2,1)S(1)}, bf16[1,128,1792]{2,1,0:T(8,128)(2,1)}, u32[]{:S(2)}) copy-start(bf16[1,128,1792]{2,1,0:T(8,128)(2,1)} %get-tuple-element.10) | copy-start | bytes 1376260
  204.3 1.2 copy-start

commit v2 on v1

v2 whole, which is shorter than its diff:
```python
import functools

import jax
import jax.numpy as jnp
from jax import lax
from jax.experimental import pallas as pl
from jax.experimental.pallas import tpu as pltpu
from jax.sharding import PartitionSpec as P

MESH = pl.DeviceIdType.MESH
BF = jnp.bfloat16
F32 = jnp.float32
NX = 4
ROWS = 128
CW = 128
SA = 2
SZ = 2
SR = 2
XF = 2 * SA
WA, WZ, WR = 2 * SA + 2, 2 * SZ + 2, 2 * SR + 2
FIRST = ((0, 2), (2, 6), (6, 14))


def kernel(
    nch, x_hbm, gw_hbm, uw_hbm, cot_hbm, hid_hbm, dx_hbm, gg_hbm, ug_hbm,
    hid_ref, dx_ref, gg_ref, ug_ref, panel, gpart, rb0, rb1, rb2, rb3, xp, xt, acc, part, zin, dl, cot, dxs, dxr, dxz, dxq,
    loc_sem, in_sem, out_sem, first_send, first_recv, ag_send, ag_recv, rs_send, rs_recv, z_send, z_recv, x_send, x_recv, d_send, d_recv,
):
    d, r, c = lax.axis_index("depth"), lax.axis_index("row"), lax.axis_index("col")
    x, y = lax.div(d, NX), lax.rem(d, NX)
    zl, k = lax.div(c, 2), lax.rem(c, 2)
    tok = dx_ref.shape[0]
    half = tok // 2
    fb = dx_ref.shape[1]

    def ring(p, s):
        return lax.rem(p + s + NX, NX)

    def x_dev(s):
        return {"depth": ring(x, s) * NX + y}

    def y_dev(s):
        return {"depth": x * NX + ring(y, s)}

    row_dev = {"row": 1 - r}
    sib_dev = {"col": c + 1 - 2 * k}

    def z_dev(s):
        return {"col": ring(zl, s) * 2 + k}

    def remote(src, dst, ssem, rsem, dev):
        return pltpu.make_async_remote_copy(
            src_ref=src, dst_ref=dst, send_sem=ssem, recv_sem=rsem, device_id=dev, device_id_type=MESH
        )

    def cols(j):
        return pl.ds(pl.multiple_of(j * CW, CW), CW)

    def feat(b):
        return pl.ds(pl.multiple_of(b * fb, fb), fb)

    def send(make, j):
        @pl.when(j >= 2)
        def _():
            make(j - 2).wait_send()

        make(j).start()

    w_hbm = (gw_hbm, uw_hbm)

    def own(j, s):
        return pltpu.make_async_copy(w_hbm[s].at[0, :, cols(j)], panel.at[j, s, x, y], loc_sem.at[s, j])

    own_x = pltpu.make_async_copy(x_hbm, xp.at[:, feat(c)], in_sem.at[0])
    own_cot = pltpu.make_async_copy(cot_hbm, cot, in_sem.at[1])

    def start_own(j, carry):
        for s in range(2):
            own(j, s).start()
        return carry

    own_x.start()
    lax.fori_loop(0, nch, start_own, 0)
    own_cot.start()

    partners = [x_dev(1), x_dev(-1), y_dev(1), y_dev(-1), row_dev, sib_dev, z_dev(1), z_dev(2), z_dev(3)]
    barrier = pltpu.get_barrier_semaphore()
    for dev in partners:
        pl.semaphore_signal(barrier, inc=1, device_id=dev, device_id_type=MESH)
    pl.semaphore_wait(barrier, len(partners))

    def x_line(s, b):
        blk = xp.at[:, feat(b)]
        return remote(blk, blk, x_send.at[s - 1], x_recv.at[s - 1], z_dev(s))

    def x_sib(s, b):
        blk = xp.at[:, feat(b)]
        return remote(blk, blk, x_send.at[3 + s], x_recv.at[3 + s], sib_dev)

    def x_start():
        own_x.wait()
        for s in (1, 2, 3):
            x_line(s, c).start()
        x_sib(0, c).start()

    def x_forward():
        for s in (1, 3, 2):
            b = ring(zl, -s) * 2 + k
            x_line(s, b).wait_recv()
            x_sib(s, b).start()

    def x_finish():
        for s in (1, 2, 3):
            x_line(s, c).wait_send()
        for s in range(4):
            b = ring(zl, -s) * 2 + 1 - k
            x_sib(s, b).wait_recv()
            x_sib(s, c).wait_send()
        for i in range(NX):
            w = 4 * ROWS
            xt[i] = jnp.transpose(xp[:, i * w : (i + 1) * w])

    def ring_dev(axis, s):
        return x_dev(s) if axis == 0 else y_dev(s)

    def me(axis):
        return x if axis == 0 else y

    def block(buf, j, s, p):
        return buf.at[j, 0, p, y] if s == 0 else buf.at[j, 1, x, p]

    def block_half(buf, j, s, p, h):
        rows = pl.ds(h * (ROWS // 2), ROWS // 2)
        return buf.at[j, 0, p, y, rows] if s == 0 else buf.at[j, 1, x, p, rows]

    def group(buf, j, s, q):
        return buf.at[j, 0, :, q] if s == 0 else buf.at[j, 1, q]

    def group_half(buf, j, s, q, h):
        return buf.at[j, 0, pl.ds(2 * h, 2), q] if s == 0 else buf.at[j, 1, q, pl.ds(2 * h, 2)]

    def first_part(n, s, p):
        lo, hi = FIRST[n]
        js = pl.ds(lo, hi - lo)
        return panel.at[js, 0, p, y] if s == 0 else panel.at[js, 1, x, p]

    def first(n, s, i, p):
        src = first_part(n, s, p)
        return remote(src, src, first_send.at[s, i, n], first_recv.at[s, i, n], ring_dev(s, 1 - 2 * i))

    def first_start(n):
        def ready(j, carry):
            for s in range(2):
                own(j, s).wait()
            return carry

        lax.fori_loop(*FIRST[n], ready, 0)
        for s in range(2):
            for i in range(2):
                first(n, s, i, me(s)).start()

    def first_wait(n):
        for s in range(2):
            for i in range(2):
                first(n, s, i, ring(me(s), -1 + 2 * i)).wait_recv()
        for s in range(2):
            for i in range(2):
                first(n, s, i, me(s)).wait_send()

    def ag_ref(stage, j, s, i, shift):
        if stage == 1:
            return block_half(panel, j, s, ring(me(s), shift), i)
        q = ring(me(1 - s), shift)
        return group(panel, j, s, q) if stage == 2 else group_half(panel, j, s, q, i)

    def ag(stage, j, s, i, shift):
        src = ag_ref(stage, j, s, i, shift)
        axis = s if stage == 1 else 1 - s
        return remote(
            src, src, ag_send.at[stage - 1, s, i, lax.rem(j, 2)],
            ag_recv.at[stage - 1, s, i, lax.rem(j, WA)], ring_dev(axis, 1 - 2 * i),
        )

    def ag_out(stage, s, i):
        return lambda j: ag(stage, j, s, i, 0 if stage == 2 else -1 + 2 * i)

    def ag1(j):
        for n in range(len(FIRST)):
            pl.when(j == FIRST[n][0])(functools.partial(first_wait, n))
        for s in range(2):
            for i in range(2):
                send(ag_out(1, s, i), j)

    def ag2(j):
        for s in range(2):
            for i in range(2):
                ag(1, j, s, i, 2).wait_recv()
            for i in range(2):
                send(ag_out(2, s, i), j)

    def ag3(j):
        for s in range(2):
            for i in range(2):
                ag(2, j, s, i, -1 + 2 * i).wait_recv()
                send(ag_out(3, s, i), j)

    def ag4(j):
        for s in range(2):
            for i in range(2):
                ag(3, j, s, i, 2).wait_recv()

    def z1(j):
        return remote(
            part.at[j, 1 - r], zin.at[j], z_send.at[0, lax.rem(j, 2)], z_recv.at[0, lax.rem(j, WZ)], row_dev
        )

    def z2(j, h):
        src = dl.at[j, h]
        return remote(src, src, z_send.at[1, lax.rem(j, 2)], z_recv.at[1, lax.rem(j, WZ)], row_dev)

    def z2_out(j):
        return z2(j, r)

    def weights(j, i):
        n = 4 * ROWS
        return jnp.concatenate([panel[j, 0, i].reshape(n, CW), panel[j, 1, i].reshape(n, CW)], axis=1)

    def forward(j):
        ag4(j)
        w = jnp.concatenate([weights(j, i) for i in range(NX)], axis=0)
        out = jnp.dot(xp[...], w, preferred_element_type=F32)
        part[j] = out.reshape(2, half, 2 * CW).astype(BF)
        send(z1, j)

    def deltas(j):
        z1(j).wait_recv()
        total = part[j, r].astype(F32) + zin[j].astype(F32)
        gate, up = total[:, :CW], total[:, CW:]
        sig = jax.nn.sigmoid(gate)
        act = gate * sig
        hid_ref[:, cols(j)] = (act * up).astype(BF)
        upstream = cot[:, cols(j)].astype(F32)
        gd = (upstream * up * sig * (1.0 + gate * (1.0 - sig))).astype(BF)
        ud = (upstream * act).astype(BF)
        dl[j, r] = jnp.concatenate([gd, ud], axis=1)
        send(z2_out, j)

    def grads(j):
        z2(j, 1 - r).wait_recv()

        def wgrad(i, carry):
            g = jnp.dot(xt[i], dl[j].reshape(tok, 2 * CW), preferred_element_type=F32).astype(BF)
            gpart[j, 0, i] = g[:, :CW].reshape(NX, ROWS, CW)
            gpart[j, 1, i] = g[:, CW:].reshape(NX, ROWS, CW)
            return carry

        lax.fori_loop(0, NX, wgrad, 0)
        rs0(j)

        def dgrad(i, carry):
            w = weights(j, i)
            p = lax.dot_general(
                dl[j].reshape(tok, 2 * CW), w, (((1,), (1,)), ((), ())), preferred_element_type=F32
            )
            sl = pl.ds(pl.multiple_of(i * 4 * ROWS, 4 * ROWS), 4 * ROWS)

            @pl.when(j == 0)
            def _():
                acc[:, sl] = p

            @pl.when(j > 0)
            def _():
                acc[:, sl] += p

            return carry

        lax.fori_loop(0, NX, dgrad, 0)

    def rs_ref(stage, j, s, i):
        m = me(1 - s) if stage < 2 else me(s)
        if stage == 0:
            return group_half(gpart, j, s, ring(m, 2), i)
        if stage == 1:
            return group(gpart, j, s, ring(m, 1 - 2 * i))
        if stage == 2:
            return block_half(gpart, j, s, ring(m, 2), i)
        return block(gpart, j, s, ring(m, 1 - 2 * i))

    def rs(stage, j, s, i):
        axis = 1 - s if stage < 2 else s
        dst = (rb0, rb1, rb2, rb3)[stage].at[j, s, i]
        return remote(
            rs_ref(stage, j, s, i), dst, rs_send.at[stage, s, i, lax.rem(j, 2)],
            rs_recv.at[stage, s, i, lax.rem(j, WR)], ring_dev(axis, 1 - 2 * i),
        )

    def rs_out(stage, s, i):
        return lambda j: rs(stage, j, s, i)

    def add(ref, *others):
        v = ref[...].astype(F32)
        for o in others:
            v = v + o[...].astype(F32)
        ref[...] = v.astype(BF)

    def rs0(j):
        for s in range(2):
            for i in range(2):
                send(rs_out(0, s, i), j)

    def rs1(j):
        for s in range(2):
            for i in range(2):
                rs(0, j, s, i).wait_recv()
                add(group_half(gpart, j, s, ring(me(1 - s), 1 - 2 * i), i), rb0.at[j, s, i])
                send(rs_out(1, s, i), j)

    def rs2(j):
        for s in range(2):
            for i in range(2):
                rs(1, j, s, i).wait_recv()
            add(group(gpart, j, s, me(1 - s)), rb1.at[j, s, 0], rb1.at[j, s, 1])
            for i in range(2):
                send(rs_out(2, s, i), j)

    def rs3(j):
        for s in range(2):
            for i in range(2):
                rs(2, j, s, i).wait_recv()
                add(block_half(gpart, j, s, ring(me(s), 1 - 2 * i), i), rb2.at[j, s, i])
                send(rs_out(3, s, i), j)

    def rs4(j):
        for s, out in enumerate((gg_ref, ug_ref)):
            for i in range(2):
                rs(3, j, s, i).wait_recv()
            v = block(gpart, j, s, me(s))[...].astype(F32)
            v = v + rb3[j, s, 0].astype(F32) + rb3[j, s, 1].astype(F32)
            out[0, :, cols(j)] = v.astype(BF)

    d_sib = remote(dxs, dxr, d_send.at[0], d_recv.at[0], sib_dev)

    def d_line(s):
        return remote(dxz.at[s - 1], dxq.at[s - 1], d_send.at[s], d_recv.at[s], z_dev(s))

    def dx0():
        for i in range(4):
            dxs[i] = acc[:, feat(2 * i + 1 - k)].astype(BF)
        d_sib.start()

    def dx1():
        d_sib.wait()
        for s in (2, 1, 3):
            zt = ring(zl, s)
            dxz[s - 1] = (acc[:, feat(2 * zt + k)] + dxr[zt].astype(F32)).astype(BF)
            d_line(s).start()

    def dx2():
        v = acc[:, feat(2 * zl + k)] + dxr[zl].astype(F32)
        for s in (1, 2, 3):
            d_line(s).wait()
            v = v + dxq[s - 1].astype(F32)
        dx_ref[...] = v.astype(BF)
        result(1).start()

    outs = ((hid_ref, hid_hbm), (dx_ref, dx_hbm), (gg_ref, gg_hbm), (ug_ref, ug_hbm))

    def result(n):
        return pltpu.make_async_copy(*outs[n], out_sem.at[n])

    fo = 3 * SA
    og = fo + 2 * SZ
    last = og + 4 * SR
    x_start()
    first_start(0)
    first_start(1)

    def tick(t, carry):
        def at(off, fn):
            j = t - off

            @pl.when((j >= 0) & (j < nch))
            def _():
                fn(j)

        at(2 * SA, ag3)
        at(SA, ag2)
        at(0, ag1)
        pl.when(t == SA)(functools.partial(first_start, 2))
        pl.when(t == XF)(x_forward)

        @pl.when(t == fo)
        def _():
            x_finish()
            own_cot.wait()

        at(last, rs4)
        at(og + 3 * SR, rs3)
        at(og + 2 * SR, rs2)
        at(og + SR, rs1)
        at(fo + SZ, deltas)
        at(fo, forward)
        at(og, grads)
        pl.when(t == nch - 1 + fo + SZ)(result(0).start)
        pl.when(t == nch - 1 + og)(dx0)
        pl.when(t == nch - 1 + og + SR)(dx1)
        pl.when(t == nch - 1 + og + 2 * SR)(dx2)
        return carry

    lax.fori_loop(0, nch + last, tick, 0)
    result(2).start()
    result(3).start()
    for j in (nch - 2, nch - 1):
        for s in range(2):
            for i in range(2):
                for stage in (1, 2, 3):
                    ag_out(stage, s, i)(j).wait_send()
                for stage in range(4):
                    rs(stage, j, s, i).wait_send()
        z1(j).wait_send()
        z2_out(j).wait_send()
    for n in range(4):
        result(n).wait()


def hand_on(*refs):
    ins, outs, held, in_sem, out_sem = refs[:4], refs[4:8], refs[8:12], refs[12], refs[13]
    reads = [pltpu.make_async_copy(a, b, in_sem.at[n]) for n, (a, b) in enumerate(zip(ins, held))]
    writes = [pltpu.make_async_copy(a, b, out_sem.at[n]) for n, (a, b) in enumerate(zip(held, outs))]
    for read in reads:
        read.start()
    for read, write in zip(reads, writes):
        read.wait()
        write.start()
    for write in writes:
        write.wait()


def local(inputs, gate_weight, up_weight, cotangent):
    tok, fb = inputs.shape
    _, rows, width = gate_weight.shape
    half = cotangent.shape[0]
    nch = width // CW
    feats = rows * NX * NX
    vm, dma = pltpu.VMEM, pltpu.SemaphoreType.DMA
    any_spec = pl.BlockSpec(memory_space=pl.ANY)
    shapes = ((half, width), (tok, fb), (1, rows, width), (1, rows, width))
    out_shape = tuple(jax.ShapeDtypeStruct(shape, BF) for shape in shapes)
    results = pl.pallas_call(
        functools.partial(kernel, nch),
        out_shape=out_shape,
        in_specs=[any_spec] * 4,
        out_specs=[any_spec] * 4,
        scratch_shapes=[
            *(vm(shape, BF) for shape in shapes),
            vm((nch, 2, NX, NX, rows, CW), BF),
            vm((nch, 2, NX, NX, rows, CW), BF),
            vm((nch, 2, 2, 2, rows, CW), BF),
            vm((nch, 2, 2, NX, rows, CW), BF),
            vm((nch, 2, 2, rows // 2, CW), BF),
            vm((nch, 2, 2, rows, CW), BF),
            vm((tok, feats), BF),
            vm((NX, 4 * rows, tok), BF),
            vm((tok, feats), F32),
            vm((nch, 2, half, 2 * CW), BF),
            vm((nch, half, 2 * CW), BF),
            vm((nch, 2, half, 2 * CW), BF),
            vm((half, width), BF),
            vm((4, tok, fb), BF),
            vm((4, tok, fb), BF),
            vm((3, tok, fb), BF),
            vm((3, tok, fb), BF),
            dma((2, nch)),
            dma((2,)),
            dma((4,)),
            dma((2, 2, len(FIRST))),
            dma((2, 2, len(FIRST))),
            dma((3, 2, 2, 2)),
            dma((3, 2, 2, WA)),
            dma((4, 2, 2, 2)),
            dma((4, 2, 2, WR)),
            dma((2, 2)),
            dma((2, WZ)),
            dma((7,)),
            dma((7,)),
            dma((4,)),
            dma((4,)),
        ],
        compiler_params=pltpu.CompilerParams(
            collective_id=0, has_side_effects=True, vmem_limit_bytes=62 * 2**20
        ),
    )(inputs, gate_weight, up_weight, cotangent)
    return pl.pallas_call(
        hand_on,
        out_shape=out_shape,
        in_specs=[any_spec] * 4,
        out_specs=[any_spec] * 4,
        scratch_shapes=[*(vm(shape, BF) for shape in shapes), dma((4,)), dma((4,))],
    )(*results)


def solution(mesh):
    return jax.shard_map(
        local,
        mesh=mesh,
        in_specs=(
            P("depth", ("row", "col")),
            P("row", "depth", "col"),
            P("row", "depth", "col"),
            P(("depth", "row"), "col"),
        ),
        out_specs=(
            P(("depth", "row"), "col"),
            P("depth", ("row", "col")),
            P("row", "depth", "col"),
            P("row", "depth", "col"),
        ),
        check_vma=False,
    )
```

time: 206 us -> 172 us (0.83)
  Pallas kernels: 201 us -> 171 us
  local copies, waits for them, and re-layouts: 4.54 us -> 0 us
    pallas_call x1 -> x2, Pallas kernels: 201 us -> 171 us  [the longest x1 169 us: local(): pl.pallas_call(functools.partial(kernel, nch), out_shape=out_shape, in_sp...]
    unnamed x10 -> x0, local copies, waits for them, and re-layouts: 4.54 us -> none
where the time goes in v2:
time: 172 us
  Pallas kernels  171 us (99%)
    pallas_call x1, Pallas kernels, local(): pl.pallas_call(functools.partial(kernel, nch), out_shape=out_shape, in_sp...  169 us

profile of v2, /device:TPU:32, one launch (start us, length us, event | category | flops | bytes accessed | tf_op | source)
XLA Modules:
  0.0 171.6 jit_solution(799164627581676772)
XLA Ops:
  0.6 168.7 %shard_map.75 = (bf16[144,1792]{1,0:T(8,128)(2,1)}, bf16[288,256]{1,0:T(8,128)(2,1)}, bf16[1,128,1792]{2,1,0:T(8,128)(2,1)}, bf16[1,128,1792]{2,1,0:T(8,128)(2,1)}) custom-call(bf16[288,256]{1,0:T(8,128)(2,1)} %x_hbm.1, bf16[1,128,1792]{2,1,0:T(8,128)(2,1)} %gw_hbm.1, bf16[1,128,1792]{2,1,0:T(8,128)(2,1)} %uw_hbm.1, bf16[144,1792]{1,0:T(8,128)(2,1)} %cot_hbm.1), custom_call_target="tpu_custom_call" | custom-call | tf_op jit(solution)/shard_map/pallas_call | solution.py:449
  169.4 2.2 %shard_map.76 = (bf16[144,1792]{1,0:T(8,128)(2,1)}, bf16[288,256]{1,0:T(8,128)(2,1)}, bf16[1,128,1792]{2,1,0:T(8,128)(2,1)}, bf16[1,128,1792]{2,1,0:T(8,128)(2,1)}) custom-call(bf16[144,1792]{1,0:T(8,128)(2,1)} %get-tuple-element.8.refs_0_, bf16[288,256]{1,0:T(8,128)(2,1)} %get-tuple-element.9.refs_1_, bf16[1,128,1792]{2,1,0:T(8,128)(2,1)} %get-tuple-element.10.refs_2_, ...), custom_call_target="tpu_custom_call" | custom-call | tf_op jit(solution)/shard_map/pallas_call | solution.py:493

commit v3 on v0

v3 whole, which is shorter than its diff:
```python
import functools

import jax
import jax.numpy as jnp
from jax import lax
from jax.experimental import pallas as pl
from jax.experimental.pallas import tpu as pltpu
from jax.sharding import PartitionSpec as P

MESH = pl.DeviceIdType.MESH
BF = jnp.bfloat16
F32 = jnp.float32
NX = 4
ROWS = 128
CW = 128
NT = 4
ORDER = (
    (0, 0), (0, 1), (1, 1), (2, 1), (3, 1), (3, 0), (0, 2), (1, 2), (2, 2), (0, 3), (1, 3), (2, 3), (1, 0), (2, 0),
)
UNITS = len(ORDER)
TILES = sum(n << 2 * u for u, (n, _) in enumerate(ORDER))
SHIFTS = sum((0, 2, 1, 3)[m] << 2 * u for u, (_, m) in enumerate(ORDER))
FIRST_OF_TILE = [min(u for u, (n, _) in enumerate(ORDER) if n == i) for i in range(NT)]
LAST_OF_TILE = [max(u for u, (n, _) in enumerate(ORDER) if n == i) for i in range(NT)]
FIRST_OF_GROUP = [min(u for u, (_, m) in enumerate(ORDER) if m == i) for i in range(4)]
LAST_OF_GROUP = [max(u for u, (_, m) in enumerate(ORDER) if m == i) for i in range(4)]
OFF = (2, 1, -1)
SD = 2
SG = 1


def kernel(
    x_hbm, gw_hbm, uw_hbm, cot_hbm, hid_hbm, dx_hbm, gg_hbm, ug_hbm,
    hid, dx, gg, ug, wpk, panel, xp, xt, acc, gacc, gp, rb0, rb1, gr, part, zin, dl, ctb, hb,
    dxs, dxr, dys, dyr, dxz, dxq,
    in_sem, own_sem, out_sem, wa_s, wa_r, wx_s, wx_r, xz_s, xz_r, xy_s, xy_r, xs_s, xs_r, ct_s, ct_r,
    z_s, z_r, rs_s, rs_r, ga_s, ga_r, hd_s, hd_r, ds_s, ds_r, dy_s, dy_r, dz_s, dz_r,
):
    d, r, c = lax.axis_index("depth"), lax.axis_index("row"), lax.axis_index("col")
    x, y = lax.div(d, NX), lax.rem(d, NX)
    zl, k = lax.div(c, 2), lax.rem(c, 2)
    tok, fb = dx.shape
    half = tok // 2

    def ring(p, s):
        return lax.rem(p + s + NX, NX)

    def x_dev(s):
        return {"depth": ring(x, s) * NX + y}

    def y_dev(s):
        return {"depth": x * NX + ring(y, s)}

    row_dev = {"row": 1 - r}
    sib_dev = {"col": c + 1 - 2 * k}

    def z_dev(s):
        return {"col": ring(zl, s) * 2 + k}

    def remote(src, dst, ssem, rsem, dev):
        return pltpu.make_async_remote_copy(
            src_ref=src, dst_ref=dst, send_sem=ssem, recv_sem=rsem, device_id=dev, device_id_type=MESH
        )

    def span(start, n):
        return pl.ds(pl.multiple_of(start * CW, CW), n * CW)

    def first_tile(q):
        return 3 * q + lax.div(q + 1, 2)

    def shared_tile(q):
        return 3 + 7 * lax.div(q, 2)

    def tile_of(q, n):
        return first_tile(q) + n if n < NT - 1 else shared_tile(q)

    def feat(b):
        return pl.ds(pl.multiple_of(b * fb, fb), fb)

    def own(n, s):
        src = (gw_hbm, uw_hbm)[s].at[0, :, span(n, 1)]
        return pltpu.make_async_copy(src, wpk.at[n, :, s * CW : (s + 1) * CW], in_sem.at[1])

    def own_start(n, carry):
        for s in range(2):
            own(n, s).start()
        return carry

    def own_tile(n):
        return pltpu.make_async_copy(wpk.at[tile_of(y, n)], panel.at[n, x, y], own_sem.at[n])

    own_x = pltpu.make_async_copy(x_hbm, xp.at[y, k, :, feat(zl)], in_sem.at[0])
    own_cot = (
        pltpu.make_async_copy(cot_hbm.at[:, span(first_tile(y), 3)], ctb.at[y, :, 0 : 3 * CW], in_sem.at[2]),
        pltpu.make_async_copy(cot_hbm.at[:, span(shared_tile(y), 1)], ctb.at[y, :, 3 * CW :], in_sem.at[3]),
    )
    own_x.start()
    lax.fori_loop(0, wpk.shape[0], own_start, 0)
    for copy in own_cot:
        copy.start()

    partners = [x_dev(1), x_dev(-1), y_dev(1), y_dev(-1), y_dev(2), row_dev, sib_dev, z_dev(1), z_dev(2), z_dev(3)]
    barrier = pltpu.get_barrier_semaphore()
    for dev in partners:
        pl.semaphore_signal(barrier, inc=1, device_id=dev, device_id_type=MESH)
    pl.semaphore_wait(barrier, len(partners))

    def wa(q, n, to, frm):
        return remote(wpk.at[tile_of(to, n)], panel.at[n, x, frm], wa_s.at[q, n], wa_r.at[q, n], y_dev(OFF[q]))

    def wa_start(n):
        own_tile(n).start()
        for q in range(3):
            wa(q, n, ring(y, OFF[q]), y).start()

    def wx(stage, n, i, shift):
        p = ring(x, shift)
        src = panel.at[n, p] if stage == 0 else panel.at[n, p, pl.ds(2 * i, 2)]
        return remote(src, src, wx_s.at[stage, i, n], wx_r.at[stage, i, n], x_dev(1 - 2 * i))

    def wg1(n):
        own_tile(n).wait()
        for q in range(3):
            wa(q, n, y, ring(y, -OFF[q])).wait_recv()
        for i in range(2):
            wx(0, n, i, 0).start()

    def wg2(n):
        for i in range(2):
            wx(0, n, i, -1 + 2 * i).wait_recv()
            wx(1, n, i, -1 + 2 * i).start()

    def wg3(n):
        for i in range(2):
            wx(1, n, i, 2).wait_recv()

    def x_line(s, b):
        blk = xp.at[y, k, :, feat(b)]
        return remote(blk, blk, xz_s.at[s - 1], xz_r.at[s - 1], z_dev(s))

    def x_side(q, n, g):
        blk = xp.at[g, k, :, feat(ring(zl, -n))]
        return remote(blk, blk, xy_s.at[q, n], xy_r.at[q, n], y_dev(OFF[q]))

    def x_sib(n, g, h):
        blk = xp.at[g, h]
        return remote(blk, blk, xs_s.at[n], xs_r.at[n], sib_dev)

    def x_whole(q, g):
        blk = xp.at[g, k]
        return remote(blk, blk, xy_s.at[q, 0], xy_r.at[q, 0], y_dev(OFF[q]))

    def x_arrive(s):
        x_line(s, ring(zl, -s)).wait_recv()
        x_side(0, s, y).start()

    def x_rest():
        for q in (2, 1):
            x_whole(q, y).start()
            ct(q, ring(y, OFF[q]), y).start()

    def x_from(q):
        return ring(y, -OFF[q])

    def x_group(q):
        g = x_from(q)
        if q == 0:
            for n in range(4):
                x_side(q, n, g).wait_recv()
        else:
            x_whole(q, g).wait_recv()
        x_sib(q + 1, g, k).start()

    def x_ready(n, g):
        x_sib(n, g, 1 - k).wait_recv()
        for i in range(NX):
            w = slice(i * fb, (i + 1) * fb)
            xt[g, i] = jnp.concatenate([jnp.transpose(xp[g, 0, :, w]), jnp.transpose(xp[g, 1, :, w])], axis=0)

    def ct(q, to, frm):
        return remote(
            cot_hbm.at[:, span(first_tile(to), 3)], ctb.at[frm, :, 0 : 3 * CW], ct_s.at[q], ct_r.at[q], y_dev(OFF[q])
        )

    def ct_shared(to, frm):
        return remote(
            cot_hbm.at[:, span(shared_tile(to), 1)], ctb.at[frm, :, 3 * CW :], ct_s.at[3], ct_r.at[3], y_dev(2)
        )

    def ct_wait(q):
        if q == 0:
            for copy in own_cot:
                copy.wait()
            ct_shared(y, ring(y, 2)).wait_recv()
        ct(q, y, ring(y, -OFF[q])).wait_recv()

    def unit(u):
        n = lax.rem(lax.shift_right_logical(jnp.int32(TILES), 2 * u), 4)
        shift = lax.rem(lax.shift_right_logical(jnp.int32(SHIFTS), 2 * u), 4)
        return n, lax.rem(y + shift, NX)

    def among(u, units):
        hit = u == units[0]
        for v in units[1:]:
            hit = hit | (u == v)
        return hit

    def z1(u):
        return remote(part.at[u, 1 - r], zin.at[u], z_s.at[0, u], z_r.at[0, u], row_dev)

    def z2(u, h):
        blk = dl.at[u, h]
        return remote(blk, blk, z_s.at[1, u], z_r.at[1, u], row_dev)

    def forward(u):
        n, g = unit(u)
        out = jnp.zeros((tok, 2 * CW), F32)
        for h in range(2):
            w = panel[n, :, 2 * h : 2 * h + 2].reshape(NX * 2 * ROWS, 2 * CW)
            out = out + jnp.dot(xp[g, h], w, preferred_element_type=F32)
        part[u] = out.reshape(2, half, 2 * CW).astype(BF)
        z1(u).start()

    def deltas(u):
        n, g = unit(u)
        z1(u).wait()
        total = part[u, r].astype(F32) + zin[u].astype(F32)
        gate, up = total[:, :CW], total[:, CW:]
        sig = jax.nn.sigmoid(gate)
        act = gate * sig
        hb[g, :, span(n, 1)] = (act * up).astype(BF)
        upstream = ctb[g, :, span(n, 1)].astype(F32)
        gd = (upstream * up * sig * (1.0 + gate * (1.0 - sig))).astype(BF)
        ud = (upstream * act).astype(BF)
        dl[u, r] = jnp.concatenate([gd, ud], axis=1)
        z2(u, r).start()

    def grads(u):
        n, g = unit(u)
        z2(u, 1 - r).wait_recv()
        z2(u, r).wait_send()
        new_tile = among(u, FIRST_OF_TILE)
        new_group = among(u, FIRST_OF_GROUP)

        def wgrad(i, carry):
            v = jnp.dot(xt[g, i], dl[u].reshape(tok, 2 * CW), preferred_element_type=F32)

            @pl.when(new_tile)
            def _():
                gacc[n, i] = v

            @pl.when(jnp.logical_not(new_tile))
            def _():
                gacc[n, i] += v

            return carry

        lax.fori_loop(0, NX, wgrad, 0)

        @pl.when(among(u, LAST_OF_TILE))
        def _():
            def cast(i, carry):
                gp[n, i] = gacc[n, i].reshape(NX, ROWS, 2 * CW).astype(BF)
                return carry

            lax.fori_loop(0, NX, cast, 0)
            for i in range(2):
                rs(0, n, i).start()

        def dgrad(i, carry):
            w = panel[n, i].reshape(NX * ROWS, 2 * CW)
            v = lax.dot_general(
                dl[u].reshape(tok, 2 * CW), w, (((1,), (1,)), ((), ())), preferred_element_type=F32
            )
            sl = pl.ds(pl.multiple_of(i * NX * ROWS, NX * ROWS), NX * ROWS)

            @pl.when(new_group)
            def _():
                acc[g, :, sl] = v

            @pl.when(jnp.logical_not(new_group))
            def _():
                acc[g, :, sl] += v

            return carry

        lax.fori_loop(0, NX, dgrad, 0)

    def rs(stage, n, i):
        src = gp.at[n, ring(x, 2), pl.ds(2 * i, 2)] if stage == 0 else gp.at[n, ring(x, 1 - 2 * i)]
        dst = (rb0, rb1)[stage].at[n, i]
        return remote(src, dst, rs_s.at[stage, i, n], rs_r.at[stage, i, n], x_dev(1 - 2 * i))

    def add(ref, *others):
        v = ref[...].astype(F32)
        for o in others:
            v = v + o[...].astype(F32)
        ref[...] = v.astype(BF)

    def rs1(n):
        for i in range(2):
            rs(0, n, i).wait()
            add(gp.at[n, ring(x, 1 - 2 * i), pl.ds(2 * i, 2)], rb0.at[n, i])
            rs(1, n, i).start()

    def ga(q, n, to, frm):
        return remote(gp.at[n, x, to], gr.at[frm, n], ga_s.at[q, n], ga_r.at[q, n], y_dev(OFF[q]))

    def rs2(n):
        for i in range(2):
            rs(1, n, i).wait()
        add(gp.at[n, x], rb1.at[n, 0], rb1.at[n, 1])
        for q in range(3):
            ga(q, n, ring(y, OFF[q]), y).start()
        gr[y, n] = gp[n, x, y]

    def rs3(n):
        for q in range(3):
            ga(q, n, y, ring(y, -OFF[q])).wait_recv()

        if n < NT - 1:
            for p in range(NX):
                at = slice((3 * p + (p + 1) // 2 + n) * CW, (3 * p + (p + 1) // 2 + n + 1) * CW)
                gg[0, :, at] = gr[p, n, :, :CW]
                ug[0, :, at] = gr[p, n, :, CW:]
        else:
            for p in range(2):
                v = (gr[2 * p, n].astype(F32) + gr[2 * p + 1, n].astype(F32)).astype(BF)
                at = slice((3 + 7 * p) * CW, (4 + 7 * p) * CW)
                gg[0, :, at] = v[:, :CW]
                ug[0, :, at] = v[:, CW:]

    def hd(q, g, frm):
        return remote(
            hb.at[g, :, 0 : 3 * CW], hid.at[:, span(first_tile(frm), 3)], hd_s.at[q], hd_r.at[q], y_dev(OFF[q])
        )

    def hd_shared(g, frm):
        return remote(
            hb.at[g, :, 3 * CW :], hid.at[:, span(shared_tile(frm), 1)], hd_s.at[3], hd_r.at[3], y_dev(2)
        )

    def hidden(q):
        hd(q, ring(y, OFF[q]), y).start()
        if q == 0:
            hd_shared(ring(y, 2), y).start()

    def hidden_own():
        hid[:, span(first_tile(y), 3)] = hb[y, :, 0 : 3 * CW]
        hid[:, span(shared_tile(y), 1)] = hb[y, :, 3 * CW :]

    def hidden_end():
        for q in range(3):
            hd(q, y, ring(y, -OFF[q])).wait_recv()
        hd_shared(y, ring(y, 2)).wait_recv()
        result(0).start()

    def d_sib(m):
        return remote(dxs.at[m], dxr.at[m], ds_s.at[m], ds_r.at[m], sib_dev)

    def d_side(q):
        return remote(dys.at[q], dyr.at[q], dy_s.at[q], dy_r.at[q], y_dev(OFF[q]))

    def d_line(s):
        return remote(dxz.at[s - 1], dxq.at[s - 1], dz_s.at[s - 1], dz_r.at[s - 1], z_dev(s))

    def group_at(m):
        return y if m == 0 else ring(y, OFF[m - 1])

    def dx0(m):
        for i in range(NX):
            dxs[m, i] = acc[group_at(m), :, feat(2 * i + 1 - k)].astype(BF)
        d_sib(m).start()

    def dx1(m):
        d_sib(m).wait()
        for i in range(NX):
            dys[m - 1, i] = (acc[group_at(m), :, feat(2 * i + k)] + dxr[m, i].astype(F32)).astype(BF)
        d_side(m - 1).start()

    def dx_sum(b):
        v = acc[y, :, feat(2 * b + k)] + dxr[0, b].astype(F32)
        for q in range(3):
            v = v + dyr[q, b].astype(F32)
        return v

    def dx2():
        d_sib(0).wait()
        for q in range(3):
            d_side(q).wait()
        for s in (2, 1, 3):
            dxz[s - 1] = dx_sum(ring(zl, s)).astype(BF)
            d_line(s).start()

    def dx3():
        v = dx_sum(zl)
        for s in (1, 2, 3):
            d_line(s).wait()
            v = v + dxq[s - 1].astype(F32)
        dx[...] = v.astype(BF)
        result(1).start()

    outs = ((hid, hid_hbm), (dx, dx_hbm), (gg, gg_hbm), (ug, ug_hbm))

    def result(n):
        return pltpu.make_async_copy(*outs[n], out_sem.at[n])

    own_x.wait()
    for s in (2, 1, 3):
        x_line(s, zl).start()
    pltpu.make_async_copy(wpk, wpk, in_sem.at[1]).wait()
    wa_start(0)
    x_side(0, 0, y).start()
    wa_start(1)
    wg1(0)
    x_arrive(1)
    wa_start(2)
    wg2(0)
    x_arrive(3)
    wg1(1)
    x_arrive(2)
    x_sib(0, y, k).start()
    ct(0, ring(y, 2), y).start()
    ct_shared(ring(y, 2), y).start()
    wa_start(3)
    wg3(0)
    x_ready(0, y)

    og = SD + SG

    def tick(t, carry):
        def on(at, fn, *args):
            pl.when(t == at)(functools.partial(fn, *args))

        def at(off, fn):
            u = t - off

            @pl.when((u >= 0) & (u < UNITS))
            def _():
                fn(u)

        on(SD, ct_wait, 0)
        on(SD + FIRST_OF_GROUP[2], ct_wait, 2)
        on(SD + FIRST_OF_GROUP[3], ct_wait, 1)
        at(SD, deltas)
        on(1, x_ready, 1, ring(y, 2))
        on(2, wg3, 1)
        on(3, wg3, 2)
        on(4, wg3, 3)
        on(FIRST_OF_GROUP[2], x_ready, 3, ring(y, 1))
        on(FIRST_OF_GROUP[3], x_ready, 2, ring(y, -1))
        at(0, forward)
        on(0, wg2, 1)
        on(0, wg1, 2)
        on(0, x_group, 0)
        on(0, x_rest)
        on(1, wg2, 2)
        on(1, wg1, 3)
        on(3, wg2, 3)
        on(FIRST_OF_GROUP[2] - 2, x_group, 2)
        on(FIRST_OF_GROUP[3] - 2, x_group, 1)
        at(og, grads)
        for m in range(4):
            on(og + LAST_OF_GROUP[m], dx0, m)
        on(SD + LAST_OF_GROUP[0], hidden_own)
        for q in range(3):
            on(SD + LAST_OF_GROUP[q + 1], hidden, q)
        for m in range(1, 4):
            on(og + LAST_OF_GROUP[m] + 1, dx1, m)
        on(og + LAST_OF_GROUP[0] + 1, dx2)
        for n, u in enumerate(LAST_OF_TILE):
            on(og + u + 3, rs3, n)
        for n, u in enumerate(LAST_OF_TILE):
            on(og + u + 2, rs2, n)
        for n, u in enumerate(LAST_OF_TILE):
            on(og + u + 1, rs1, n)
        on(og + UNITS + 1, hidden_end)
        on(og + UNITS + 2, dx3)
        return carry

    lax.fori_loop(0, og + UNITS + 3, tick, 0)
    result(2).start()
    result(3).start()
    for n in range(NT):
        for q in range(3):
            wa(q, n, ring(y, OFF[q]), y).wait_send()
            ga(q, n, ring(y, OFF[q]), y).wait_send()
        for i in range(2):
            wx(0, n, i, 0).wait_send()
            wx(1, n, i, -1 + 2 * i).wait_send()
        x_sib(n, y, k).wait_send()
        x_side(0, n, y).wait_send()
    for q in range(3):
        x_line(q + 1, zl).wait_send()
        ct(q, ring(y, OFF[q]), y).wait_send()
        hd(q, ring(y, OFF[q]), y).wait_send()
    ct_shared(ring(y, 2), y).wait_send()
    x_whole(1, y).wait_send()
    x_whole(2, y).wait_send()
    hd_shared(ring(y, 2), y).wait_send()
    for n in range(4):
        result(n).wait()


def hand_on(*refs):
    ins, outs, held, in_sem, out_sem = refs[:4], refs[4:8], refs[8:12], refs[12], refs[13]
    reads = [pltpu.make_async_copy(a, b, in_sem.at[n]) for n, (a, b) in enumerate(zip(ins, held))]
    writes = [pltpu.make_async_copy(a, b, out_sem.at[n]) for n, (a, b) in enumerate(zip(held, outs))]
    for read in reads:
        read.start()
    for read, write in zip(reads, writes):
        read.wait()
        write.start()
    for write in writes:
        write.wait()


def local(inputs, gate_weight, up_weight, cotangent):
    tok, fb = inputs.shape
    _, rows, width = gate_weight.shape
    half = cotangent.shape[0]
    feats = rows * NX * NX
    vm, dma = pltpu.VMEM, pltpu.SemaphoreType.DMA
    any_spec = pl.BlockSpec(memory_space=pl.ANY)
    shapes = ((half, width), (tok, fb), (1, rows, width), (1, rows, width))
    out_shape = tuple(jax.ShapeDtypeStruct(shape, BF) for shape in shapes)
    results = pl.pallas_call(
        kernel,
        out_shape=out_shape,
        in_specs=[any_spec] * 4,
        out_specs=[any_spec] * 4,
        scratch_shapes=[
            *(vm(shape, BF) for shape in shapes),
            vm((width // CW, rows, 2 * CW), BF),
            vm((NT, NX, NX, rows, 2 * CW), BF),
            vm((NX, 2, tok, feats // 2), BF),
            vm((NX, NX, NX * rows, tok), BF),
            vm((NX, tok, feats), F32),
            vm((NT, NX, NX * rows, 2 * CW), F32),
            vm((NT, NX, NX, rows, 2 * CW), BF),
            vm((NT, 2, 2, rows, 2 * CW), BF),
            vm((NT, 2, NX, rows, 2 * CW), BF),
            vm((NX, NT, rows, 2 * CW), BF),
            vm((UNITS, 2, half, 2 * CW), BF),
            vm((UNITS, half, 2 * CW), BF),
            vm((UNITS, 2, half, 2 * CW), BF),
            vm((NX, half, NT * CW), BF),
            vm((NX, half, NT * CW), BF),
            vm((4, 4, tok, fb), BF),
            vm((4, 4, tok, fb), BF),
            vm((3, 4, tok, fb), BF),
            vm((3, 4, tok, fb), BF),
            vm((3, tok, fb), BF),
            vm((3, tok, fb), BF),
            dma((4,)),
            dma((NT,)),
            dma((4,)),
            *(dma((3, NT)) for _ in range(2)),
            *(dma((2, 2, NT)) for _ in range(2)),
            *(dma((3,)) for _ in range(2)),
            *(dma((3, 4)) for _ in range(2)),
            *(dma((4,)) for _ in range(2)),
            *(dma((4,)) for _ in range(2)),
            *(dma((2, UNITS)) for _ in range(2)),
            *(dma((2, 2, NT)) for _ in range(2)),
            *(dma((3, NT)) for _ in range(2)),
            *(dma((4,)) for _ in range(2)),
            *(dma((4,)) for _ in range(2)),
            *(dma((3,)) for _ in range(2)),
            *(dma((3,)) for _ in range(2)),
        ],
        compiler_params=pltpu.CompilerParams(
            collective_id=0, has_side_effects=True, vmem_limit_bytes=62 * 2**20
        ),
    )(inputs, gate_weight, up_weight, cotangent)
    return pl.pallas_call(
        hand_on,
        out_shape=out_shape,
        in_specs=[any_spec] * 4,
        out_specs=[any_spec] * 4,
        scratch_shapes=[*(vm(shape, BF) for shape in shapes), dma((4,)), dma((4,))],
    )(*results)


def solution(mesh):
    return jax.shard_map(
        local,
        mesh=mesh,
        in_specs=(
            P("depth", ("row", "col")),
            P("row", "depth", "col"),
            P("row", "depth", "col"),
            P(("depth", "row"), "col"),
        ),
        out_specs=(
            P(("depth", "row"), "col"),
            P("depth", ("row", "col")),
            P("row", "depth", "col"),
            P("row", "depth", "col"),
        ),
        check_vma=False,
    )
```

time: 512 us -> 165 us (0.32)
  waiting for transfers between devices: 380 us -> 0 us
  Pallas kernels: 0 us -> 164 us
  blocking collectives: 51.4 us -> 0 us
  matrix products: 36 us -> 0 us
  local copies, waits for them, and re-layouts: 22.5 us -> 0 us
  between operations: 14.2 us -> 0.64 us
    all_gather x3 -> x0, waiting for transfers between devices: 176 us -> none  [the longest x1 74.1 us: local(): lax.all_gather(up_weight, 'depth', axis=1, tiled=True)]
    pallas_call x0 -> x2, Pallas kernels: none -> 164 us  [the longest x1 162 us: local(): pl.pallas_call(kernel, out_shape=out_shape, in_specs=[any_spec] * 4, out_...]
    reduce_scatter x3 -> x0, waiting for transfers between devices: 107 us -> none  [the longest x1 39.4 us: local(): lax.psum_scatter(gate_part.astype(jnp.bfloat16), 'row', scatter_dimension...]
    unnamed x8 -> x0, waiting for transfers between devices: 97.2 us -> none
    all_gather x2 -> x0, blocking collectives: 51.4 us -> none  [the longest x1 27.4 us: local(): lax.all_gather(gate_share, 'row', axis=0, tiled=True)]
    dot_general x5 -> x0, matrix products: 36 us -> none  [the longest x1 11.1 us: local(): lax.dot_general(panel, deltas, (((0,), (0,)), ((), ())), preferred_elemen...]
    unnamed x9 -> x0, local copies, waits for them, and re-layouts: 21.3 us -> none
  transfers between devices with their start and end apart: 7 -> 0, of which waited for: 7 -> 0; matrix products, arithmetic and copies ran while one was open for 6% -> 0% of each run, Pallas kernels for 0% -> 0%
where the time goes in v3:
time: 165 us
  Pallas kernels  164 us (99%)
    pallas_call x1, Pallas kernels, local(): pl.pallas_call(kernel, out_shape=out_shape, in_specs=[any_spec] * 4, out_...  162 us

profile of v3, /device:TPU:32, one launch (start us, length us, event | category | flops | bytes accessed | tf_op | source)
XLA Modules:
  0.0 164.6 jit_solution(9810710999651790585)
XLA Ops:
  0.6 161.7 %shard_map.75 = (bf16[144,1792]{1,0:T(8,128)(2,1)}, bf16[288,256]{1,0:T(8,128)(2,1)}, bf16[1,128,1792]{2,1,0:T(8,128)(2,1)}, bf16[1,128,1792]{2,1,0:T(8,128)(2,1)}) custom-call(bf16[288,256]{1,0:T(8,128)(2,1)} %x_hbm.1, bf16[1,128,1792]{2,1,0:T(8,128)(2,1)} %gw_hbm.1, bf16[1,128,1792]{2,1,0:T(8,128)(2,1)} %uw_hbm.1, bf16[144,1792]{1,0:T(8,128)(2,1)} %cot_hbm.1), custom_call_target="tpu_custom_call" | custom-call | tf_op jit(solution)/shard_map/pallas_call | solution.py:527
  162.4 2.2 %shard_map.76 = (bf16[144,1792]{1,0:T(8,128)(2,1)}, bf16[288,256]{1,0:T(8,128)(2,1)}, bf16[1,128,1792]{2,1,0:T(8,128)(2,1)}, bf16[1,128,1792]{2,1,0:T(8,128)(2,1)}) custom-call(bf16[144,1792]{1,0:T(8,128)(2,1)} %get-tuple-element.8.refs_0_, bf16[288,256]{1,0:T(8,128)(2,1)} %get-tuple-element.9.refs_1_, bf16[1,128,1792]{2,1,0:T(8,128)(2,1)} %get-tuple-element.10.refs_2_, ...), custom_call_target="tpu_custom_call" | custom-call | tf_op jit(solution)/shard_map/pallas_call | solution.py:576

commit v4 on v3

--- a/solution.py
+++ b/solution.py
@@ -189,8 +189,6 @@
 
     def ct_wait(q):
         if q == 0:
-            for copy in own_cot:
-                copy.wait()
             ct_shared(y, ring(y, 2)).wait_recv()
         ct(q, y, ring(y, -OFF[q])).wait_recv()
 
@@ -241,31 +239,32 @@
         z2(u, r).wait_send()
         new_tile = among(u, FIRST_OF_TILE)
         new_group = among(u, FIRST_OF_GROUP)
+        last = among(u, LAST_OF_TILE)
 
         def wgrad(i, carry):
-            v = jnp.dot(xt[g, i], dl[u].reshape(tok, 2 * CW), preferred_element_type=F32)
+            p = ring(x, 2 + i)
+            v = jnp.dot(xt[g, p], dl[u].reshape(tok, 2 * CW), preferred_element_type=F32)
 
             @pl.when(new_tile)
             def _():
-                gacc[n, i] = v
+                gacc[n, p] = v
 
             @pl.when(jnp.logical_not(new_tile))
             def _():
-                gacc[n, i] += v
+                gacc[n, p] += v
+
+            @pl.when(last)
+            def _():
+                gp[n, p] = gacc[n, p].reshape(NX, ROWS, 2 * CW).astype(BF)
+
+            @pl.when(last & (i == 0))
+            def _():
+                for h in range(2):
+                    rs(0, n, h).start()
 
             return carry
 
         lax.fori_loop(0, NX, wgrad, 0)
-
-        @pl.when(among(u, LAST_OF_TILE))
-        def _():
-            def cast(i, carry):
-                gp[n, i] = gacc[n, i].reshape(NX, ROWS, 2 * CW).astype(BF)
-                return carry
-
-            lax.fori_loop(0, NX, cast, 0)
-            for i in range(2):
-                rs(0, n, i).start()
 
         def dgrad(i, carry):
             w = panel[n, i].reshape(NX * ROWS, 2 * CW)
@@ -358,8 +357,9 @@
     def d_sib(m):
         return remote(dxs.at[m], dxr.at[m], ds_s.at[m], ds_r.at[m], sib_dev)
 
-    def d_side(q):
-        return remote(dys.at[q], dyr.at[q], dy_s.at[q], dy_r.at[q], y_dev(OFF[q]))
+    def d_side(q, s):
+        b = ring(zl, s)
+        return remote(dys.at[q, b], dyr.at[q, b], dy_s.at[q, s], dy_r.at[q, s], y_dev(OFF[q]))
 
     def d_line(s):
         return remote(dxz.at[s - 1], dxq.at[s - 1], dz_s.at[s - 1], dz_r.at[s - 1], z_dev(s))
@@ -374,9 +374,10 @@
 
     def dx1(m):
         d_sib(m).wait()
-        for i in range(NX):
-            dys[m - 1, i] = (acc[group_at(m), :, feat(2 * i + k)] + dxr[m, i].astype(F32)).astype(BF)
-        d_side(m - 1).start()
+        for s in (2, 1, 3, 0):
+            b = ring(zl, s)
+            dys[m - 1, b] = (acc[group_at(m), :, feat(2 * b + k)] + dxr[m, b].astype(F32)).astype(BF)
+            d_side(m - 1, s).start()
 
     def dx_sum(b):
         v = acc[y, :, feat(2 * b + k)] + dxr[0, b].astype(F32)
@@ -386,13 +387,15 @@
 
     def dx2():
         d_sib(0).wait()
-        for q in range(3):
-            d_side(q).wait()
         for s in (2, 1, 3):
+            for q in range(3):
+                d_side(q, s).wait()
             dxz[s - 1] = dx_sum(ring(zl, s)).astype(BF)
             d_line(s).start()
 
     def dx3():
+        for q in range(3):
+            d_side(q, 0).wait()
         v = dx_sum(zl)
         for s in (1, 2, 3):
             d_line(s).wait()
@@ -410,21 +413,39 @@
         x_line(s, zl).start()
     pltpu.make_async_copy(wpk, wpk, in_sem.at[1]).wait()
     wa_start(0)
+    wa_start(1)
     x_side(0, 0, y).start()
-    wa_start(1)
+    wa_start(2)
+    wa_start(3)
     wg1(0)
     x_arrive(1)
-    wa_start(2)
     wg2(0)
+    wg1(1)
     x_arrive(3)
-    wg1(1)
     x_arrive(2)
     x_sib(0, y, k).start()
     ct(0, ring(y, 2), y).start()
     ct_shared(ring(y, 2), y).start()
-    wa_start(3)
+    for copy in own_cot:
+        copy.wait()
     wg3(0)
     x_ready(0, y)
+
+    def settle():
+        for n in range(NT):
+            for q in range(3):
+                wa(q, n, ring(y, OFF[q]), y).wait_send()
+            for i in range(2):
+                wx(0, n, i, 0).wait_send()
+                wx(1, n, i, -1 + 2 * i).wait_send()
+            x_sib(n, y, k).wait_send()
+            x_side(0, n, y).wait_send()
+        for q in range(3):
+            x_line(q + 1, zl).wait_send()
+            ct(q, ring(y, OFF[q]), y).wait_send()
+        ct_shared(ring(y, 2), y).wait_send()
+        x_whole(1, y).wait_send()
+        x_whole(2, y).wait_send()
 
     og = SD + SG
 
@@ -439,10 +460,11 @@
             def _():
                 fn(u)
 
-        on(SD, ct_wait, 0)
         on(SD + FIRST_OF_GROUP[2], ct_wait, 2)
         on(SD + FIRST_OF_GROUP[3], ct_wait, 1)
-        at(SD, deltas)
+        on(1, deltas, 0)
+        on(SD + FIRST_OF_GROUP[1], ct_wait, 0)
+        pl.when((t > SD) & (t < UNITS + SD - 1))(lambda: deltas(t - SD))
         on(1, x_ready, 1, ring(y, 2))
         on(2, wg3, 1)
         on(3, wg3, 2)
@@ -459,7 +481,11 @@
         on(3, wg2, 3)
         on(FIRST_OF_GROUP[2] - 2, x_group, 2)
         on(FIRST_OF_GROUP[3] - 2, x_group, 1)
+        for n, u in enumerate(LAST_OF_TILE):
+            if u < UNITS - 1:
+                on(og + u + 1, rs1, n)
         at(og, grads)
+        on(UNITS + SD - 2, deltas, UNITS - 1)
         for m in range(4):
             on(og + LAST_OF_GROUP[m], dx0, m)
         on(SD + LAST_OF_GROUP[0], hidden_own)
@@ -467,13 +493,13 @@
             on(SD + LAST_OF_GROUP[q + 1], hidden, q)
         for m in range(1, 4):
             on(og + LAST_OF_GROUP[m] + 1, dx1, m)
+        on(og + UNITS, rs1, ORDER[-1][0])
         on(og + LAST_OF_GROUP[0] + 1, dx2)
         for n, u in enumerate(LAST_OF_TILE):
             on(og + u + 3, rs3, n)
         for n, u in enumerate(LAST_OF_TILE):
             on(og + u + 2, rs2, n)
-        for n, u in enumerate(LAST_OF_TILE):
-            on(og + u + 1, rs1, n)
+        on(UNITS - 1, settle)
         on(og + UNITS + 1, hidden_end)
         on(og + UNITS + 2, dx3)
         return carry
@@ -481,22 +507,10 @@
     lax.fori_loop(0, og + UNITS + 3, tick, 0)
     result(2).start()
     result(3).start()
-    for n in range(NT):
-        for q in range(3):
-            wa(q, n, ring(y, OFF[q]), y).wait_send()
+    for q in range(3):
+        for n in range(NT):
             ga(q, n, ring(y, OFF[q]), y).wait_send()
-        for i in range(2):
-            wx(0, n, i, 0).wait_send()
-            wx(1, n, i, -1 + 2 * i).wait_send()
-        x_sib(n, y, k).wait_send()
-        x_side(0, n, y).wait_send()
-    for q in range(3):
-        x_line(q + 1, zl).wait_send()
-        ct(q, ring(y, OFF[q]), y).wait_send()
         hd(q, ring(y, OFF[q]), y).wait_send()
-    ct_shared(ring(y, 2), y).wait_send()
-    x_whole(1, y).wait_send()
-    x_whole(2, y).wait_send()
     hd_shared(ring(y, 2), y).wait_send()
     for n in range(4):
         result(n).wait()
@@ -566,7 +580,7 @@
             *(dma((3, NT)) for _ in range(2)),
             *(dma((4,)) for _ in range(2)),
             *(dma((4,)) for _ in range(2)),
-            *(dma((3,)) for _ in range(2)),
+            *(dma((3, 4)) for _ in range(2)),
             *(dma((3,)) for _ in range(2)),
         ],
         compiler_params=pltpu.CompilerParams(

time: 165 us -> 160 us (0.970)
  Pallas kernels: 164 us -> 159 us
    pallas_call x1, Pallas kernels: 162 us -> 157 us  [local(): pl.pallas_call(kernel, out_shape=out_shape, in_specs=[any_spec] * 4, out_...]
where the time goes in v4:
time: 160 us
  Pallas kernels  159 us (99%)
    pallas_call x1, Pallas kernels, local(): pl.pallas_call(kernel, out_shape=out_shape, in_specs=[any_spec] * 4, out_...  157 us

profile of v4, /device:TPU:32, one launch (start us, length us, event | category | flops | bytes accessed | tf_op | source)
XLA Modules:
  0.0 159.7 jit_solution(654659566290557702)
XLA Ops:
  0.6 156.8 %shard_map.75 = (bf16[144,1792]{1,0:T(8,128)(2,1)}, bf16[288,256]{1,0:T(8,128)(2,1)}, bf16[1,128,1792]{2,1,0:T(8,128)(2,1)}, bf16[1,128,1792]{2,1,0:T(8,128)(2,1)}) custom-call(bf16[288,256]{1,0:T(8,128)(2,1)} %x_hbm.1, bf16[1,128,1792]{2,1,0:T(8,128)(2,1)} %gw_hbm.1, bf16[1,128,1792]{2,1,0:T(8,128)(2,1)} %uw_hbm.1, bf16[144,1792]{1,0:T(8,128)(2,1)} %cot_hbm.1), custom_call_target="tpu_custom_call" | custom-call | tf_op jit(solution)/shard_map/pallas_call | solution.py:541
  157.4 2.2 %shard_map.76 = (bf16[144,1792]{1,0:T(8,128)(2,1)}, bf16[288,256]{1,0:T(8,128)(2,1)}, bf16[1,128,1792]{2,1,0:T(8,128)(2,1)}, bf16[1,128,1792]{2,1,0:T(8,128)(2,1)}) custom-call(bf16[144,1792]{1,0:T(8,128)(2,1)} %get-tuple-element.8.refs_0_, bf16[288,256]{1,0:T(8,128)(2,1)} %get-tuple-element.9.refs_1_, bf16[1,128,1792]{2,1,0:T(8,128)(2,1)} %get-tuple-element.10.refs_2_, ...), custom_call_target="tpu_custom_call" | custom-call | tf_op jit(solution)/shard_map/pallas_call | solution.py:590

commit v5 on v4

--- a/solution.py
+++ b/solution.py
@@ -15,7 +15,8 @@
 CW = 128
 NT = 4
 ORDER = (
-    (0, 0), (0, 1), (1, 1), (2, 1), (3, 1), (3, 0), (0, 2), (1, 2), (2, 2), (0, 3), (1, 3), (2, 3), (1, 0), (2, 0),
+    (0, 0), (0, 1), (1, 1), (2, 1), (3, 1), (3, 0), (0, 2), (0, 3), (1, 2), (1, 3),
+    (2, 2), (2, 3), (1, 0), (2, 0),
 )
 UNITS = len(ORDER)
 TILES = sum(n << 2 * u for u, (n, _) in enumerate(ORDER))
@@ -34,7 +35,7 @@
     hid, dx, gg, ug, wpk, panel, xp, xt, acc, gacc, gp, rb0, rb1, gr, part, zin, dl, ctb, hb,
     dxs, dxr, dys, dyr, dxz, dxq,
     in_sem, own_sem, out_sem, wa_s, wa_r, wx_s, wx_r, xz_s, xz_r, xy_s, xy_r, xs_s, xs_r, ct_s, ct_r,
-    z_s, z_r, rs_s, rs_r, ga_s, ga_r, hd_s, hd_r, ds_s, ds_r, dy_s, dy_r, dz_s, dz_r,
+    z_s, z_r, rs_s, rs_r, ga_s, ga_r, hd_s, hd_r, ds_s, ds_r, do_s, do_r, dy_s, dy_r, dz_s, dz_r,
 ):
     d, r, c = lax.axis_index("depth"), lax.axis_index("row"), lax.axis_index("col")
     x, y = lax.div(d, NX), lax.rem(d, NX)
@@ -241,31 +242,6 @@
         new_group = among(u, FIRST_OF_GROUP)
         last = among(u, LAST_OF_TILE)
 
-        def wgrad(i, carry):
-            p = ring(x, 2 + i)
-            v = jnp.dot(xt[g, p], dl[u].reshape(tok, 2 * CW), preferred_element_type=F32)
-
-            @pl.when(new_tile)
-            def _():
-                gacc[n, p] = v
-
-            @pl.when(jnp.logical_not(new_tile))
-            def _():
-                gacc[n, p] += v
-
-            @pl.when(last)
-            def _():
-                gp[n, p] = gacc[n, p].reshape(NX, ROWS, 2 * CW).astype(BF)
-
-            @pl.when(last & (i == 0))
-            def _():
-                for h in range(2):
-                    rs(0, n, h).start()
-
-            return carry
-
-        lax.fori_loop(0, NX, wgrad, 0)
-
         def dgrad(i, carry):
             w = panel[n, i].reshape(NX * ROWS, 2 * CW)
             v = lax.dot_general(
@@ -284,11 +260,44 @@
             return carry
 
         lax.fori_loop(0, NX, dgrad, 0)
+        for m, v in enumerate(LAST_OF_GROUP):
+            pl.when(u == v)(functools.partial(dx0, m))
+
+        def wgrad(i, carry):
+            p = ring(x, 2 + i)
+            v = jnp.dot(xt[g, p], dl[u].reshape(tok, 2 * CW), preferred_element_type=F32)
+
+            @pl.when(new_tile)
+            def _():
+                gacc[n, p] = v
+
+            @pl.when(jnp.logical_not(new_tile))
+            def _():
+                gacc[n, p] += v
+
+            @pl.when(last)
+            def _():
+                gp[n, p] = gacc[n, p].reshape(NX, ROWS, 2 * CW).astype(BF)
+
+            @pl.when(last & (i == 0))
+            def _():
+                for h in range(2):
+                    rs(0, n, h).start()
+
+            return carry
+
+        lax.fori_loop(0, NX, wgrad, 0)
+
+        @pl.when(last)
+        def _():
+            for h in range(2):
+                rs(1, n, h).start()
 
     def rs(stage, n, i):
-        src = gp.at[n, ring(x, 2), pl.ds(2 * i, 2)] if stage == 0 else gp.at[n, ring(x, 1 - 2 * i)]
-        dst = (rb0, rb1)[stage].at[n, i]
-        return remote(src, dst, rs_s.at[stage, i, n], rs_r.at[stage, i, n], x_dev(1 - 2 * i))
+        p = ring(x, 2) if stage == 0 else ring(x, 1 - 2 * i)
+        rows = pl.ds(2 * (1 - i if stage == 1 else i), 2)
+        dst = rb0.at[n, i] if stage == 0 else rb1.at[n, i, rows]
+        return remote(gp.at[n, p, rows], dst, rs_s.at[stage, i, n], rs_r.at[stage, i, n], x_dev(1 - 2 * i))
 
     def add(ref, *others):
         v = ref[...].astype(F32)
@@ -300,7 +309,7 @@
         for i in range(2):
             rs(0, n, i).wait()
             add(gp.at[n, ring(x, 1 - 2 * i), pl.ds(2 * i, 2)], rb0.at[n, i])
-            rs(1, n, i).start()
+            rs(2, n, i).start()
 
     def ga(q, n, to, frm):
         return remote(gp.at[n, x, to], gr.at[frm, n], ga_s.at[q, n], ga_r.at[q, n], y_dev(OFF[q]))
@@ -308,6 +317,7 @@
     def rs2(n):
         for i in range(2):
             rs(1, n, i).wait()
+            rs(2, n, i).wait()
         add(gp.at[n, x], rb1.at[n, 0], rb1.at[n, 1])
         for q in range(3):
             ga(q, n, ring(y, OFF[q]), y).start()
@@ -367,10 +377,18 @@
     def group_at(m):
         return y if m == 0 else ring(y, OFF[m - 1])
 
+    def d_own(s):
+        b = ring(zl, s)
+        return remote(dxs.at[0, b], dxr.at[0, b], do_s.at[s], do_r.at[s], sib_dev)
+
     def dx0(m):
-        for i in range(NX):
-            dxs[m, i] = acc[group_at(m), :, feat(2 * i + 1 - k)].astype(BF)
-        d_sib(m).start()
+        for s in (2, 1, 3, 0):
+            b = ring(zl, s)
+            dxs[m, b] = acc[group_at(m), :, feat(2 * b + 1 - k)].astype(BF)
+            if m == 0:
+                d_own(s).start()
+        if m > 0:
+            d_sib(m).start()
 
     def dx1(m):
         d_sib(m).wait()
@@ -386,14 +404,15 @@
         return v
 
     def dx2():
-        d_sib(0).wait()
         for s in (2, 1, 3):
+            d_own(s).wait()
             for q in range(3):
                 d_side(q, s).wait()
             dxz[s - 1] = dx_sum(ring(zl, s)).astype(BF)
             d_line(s).start()
 
     def dx3():
+        d_own(0).wait()
         for q in range(3):
             d_side(q, 0).wait()
         v = dx_sum(zl)
@@ -486,15 +505,13 @@
                 on(og + u + 1, rs1, n)
         at(og, grads)
         on(UNITS + SD - 2, deltas, UNITS - 1)
-        for m in range(4):
-            on(og + LAST_OF_GROUP[m], dx0, m)
         on(SD + LAST_OF_GROUP[0], hidden_own)
         for q in range(3):
             on(SD + LAST_OF_GROUP[q + 1], hidden, q)
         for m in range(1, 4):
             on(og + LAST_OF_GROUP[m] + 1, dx1, m)
+        on(og + LAST_OF_GROUP[0] + 1, dx2)
         on(og + UNITS, rs1, ORDER[-1][0])
-        on(og + LAST_OF_GROUP[0] + 1, dx2)
         for n, u in enumerate(LAST_OF_TILE):
             on(og + u + 3, rs3, n)
         for n, u in enumerate(LAST_OF_TILE):
@@ -576,8 +593,9 @@
             *(dma((4,)) for _ in range(2)),
             *(dma((4,)) for _ in range(2)),
             *(dma((2, UNITS)) for _ in range(2)),
-            *(dma((2, 2, NT)) for _ in range(2)),
+            *(dma((3, 2, NT)) for _ in range(2)),
             *(dma((3, NT)) for _ in range(2)),
+            *(dma((4,)) for _ in range(2)),
             *(dma((4,)) for _ in range(2)),
             *(dma((4,)) for _ in range(2)),
             *(dma((3, 4)) for _ in range(2)),

time: 160 us -> 158 us (0.988)
  no operation moved by 1% of the time
where the time goes in v5:
time: 158 us
  Pallas kernels  158 us (100%)
    pallas_call x1, Pallas kernels, local(): pl.pallas_call(kernel, out_shape=out_shape, in_specs=[any_spec] * 4, out_...  155 us

profile of v5, /device:TPU:32, one launch (start us, length us, event | category | flops | bytes accessed | tf_op | source)
XLA Modules:
  0.0 158.1 jit_solution(10691034174276714801)
XLA Ops:
  0.6 155.3 %shard_map.75 = (bf16[144,1792]{1,0:T(8,128)(2,1)}, bf16[288,256]{1,0:T(8,128)(2,1)}, bf16[1,128,1792]{2,1,0:T(8,128)(2,1)}, bf16[1,128,1792]{2,1,0:T(8,128)(2,1)}) custom-call(bf16[288,256]{1,0:T(8,128)(2,1)} %x_hbm.1, bf16[1,128,1792]{2,1,0:T(8,128)(2,1)} %gw_hbm.1, bf16[1,128,1792]{2,1,0:T(8,128)(2,1)} %uw_hbm.1, bf16[144,1792]{1,0:T(8,128)(2,1)} %cot_hbm.1), custom_call_target="tpu_custom_call" | custom-call | tf_op jit(solution)/shard_map/pallas_call | solution.py:558
  155.9 2.2 %shard_map.76 = (bf16[144,1792]{1,0:T(8,128)(2,1)}, bf16[288,256]{1,0:T(8,128)(2,1)}, bf16[1,128,1792]{2,1,0:T(8,128)(2,1)}, bf16[1,128,1792]{2,1,0:T(8,128)(2,1)}) custom-call(bf16[144,1792]{1,0:T(8,128)(2,1)} %get-tuple-element.8.refs_0_, bf16[288,256]{1,0:T(8,128)(2,1)} %get-tuple-element.9.refs_1_, bf16[1,128,1792]{2,1,0:T(8,128)(2,1)} %get-tuple-element.10.refs_2_, ...), custom_call_target="tpu_custom_call" | custom-call | tf_op jit(solution)/shard_map/pallas_call | solution.py:608

commit v6 on v5

--- a/solution.py
+++ b/solution.py
@@ -15,8 +15,8 @@
 CW = 128
 NT = 4
 ORDER = (
-    (0, 0), (0, 1), (1, 1), (2, 1), (3, 1), (3, 0), (0, 2), (0, 3), (1, 2), (1, 3),
-    (2, 2), (2, 3), (1, 0), (2, 0),
+    (0, 0), (0, 1), (1, 1), (2, 1), (3, 1), (3, 0), (0, 2), (0, 3), (1, 2), (2, 2),
+    (1, 3), (2, 3), (1, 0), (2, 0),
 )
 UNITS = len(ORDER)
 TILES = sum(n << 2 * u for u, (n, _) in enumerate(ORDER))

time: 158 us -> 159 us (level)
  no operation moved by 1% of the time
where the time goes in v6:
time: 159 us
  Pallas kernels  158 us (99%)
    pallas_call x1, Pallas kernels, local(): pl.pallas_call(kernel, out_shape=out_shape, in_specs=[any_spec] * 4, out_...  156 us

profile of v6, /device:TPU:32, one launch (start us, length us, event | category | flops | bytes accessed | tf_op | source)
XLA Modules:
  0.0 158.7 jit_solution(18366855255926847124)
XLA Ops:
  0.6 155.8 %shard_map.75 = (bf16[144,1792]{1,0:T(8,128)(2,1)}, bf16[288,256]{1,0:T(8,128)(2,1)}, bf16[1,128,1792]{2,1,0:T(8,128)(2,1)}, bf16[1,128,1792]{2,1,0:T(8,128)(2,1)}) custom-call(bf16[288,256]{1,0:T(8,128)(2,1)} %x_hbm.1, bf16[1,128,1792]{2,1,0:T(8,128)(2,1)} %gw_hbm.1, bf16[1,128,1792]{2,1,0:T(8,128)(2,1)} %uw_hbm.1, bf16[144,1792]{1,0:T(8,128)(2,1)} %cot_hbm.1), custom_call_target="tpu_custom_call" | custom-call | tf_op jit(solution)/shard_map/pallas_call | solution.py:558
  156.5 2.2 %shard_map.76 = (bf16[144,1792]{1,0:T(8,128)(2,1)}, bf16[288,256]{1,0:T(8,128)(2,1)}, bf16[1,128,1792]{2,1,0:T(8,128)(2,1)}, bf16[1,128,1792]{2,1,0:T(8,128)(2,1)}) custom-call(bf16[144,1792]{1,0:T(8,128)(2,1)} %get-tuple-element.8.refs_0_, bf16[288,256]{1,0:T(8,128)(2,1)} %get-tuple-element.9.refs_1_, bf16[1,128,1792]{2,1,0:T(8,128)(2,1)} %get-tuple-element.10.refs_2_, ...), custom_call_target="tpu_custom_call" | custom-call | tf_op jit(solution)/shard_map/pallas_call | solution.py:608
